TPU v7x, 512 devices: a whole 4x4x16 slice. The times are simulated.
512 devices in a mesh: cell: 32 (over z, core), rays: 16 (over y, x).
Axes of the slice: x: 4, y: 4, z: 16, core: 2. Of those that a mesh axis runs over, the one named last changes fastest.
Arguments:
- ray_code: bfloat16 [4096, 32, 256], P('rays', 'cell'), may hold values from -6 to 6
- entry_index: int32 [4096, 32], P('rays', 'cell'), may hold values from 0 to 120
- sample_count: int32 [4096, 32], P('rays', 'cell'), may hold values from 0 to 8
- step_length: float32 [4096, 32], P('rays', 'cell'), may hold values from 0.0001 to 0.75
- positions: bfloat16 [32, 128, 256], P('cell'), may hold values from -6 to 6
- w_first: bfloat16 [32, 256, 256], P('cell'), may hold values from -0.375 to 0.375
- w_second: float32 [32, 256, 256], P('cell'), may hold values from -0.375 to 0.375
- w_density: bfloat16 [32, 256], P('cell'), may hold values from -0.375 to 0.375
- w_feature: float32 [32, 256, 768], P('cell'), may hold values from -0.375 to 0.375
- mean_second: float32 [32, 256, 256], P('cell'), may hold values from -2 to 2
- square_second: float32 [32, 256, 256], P('cell'), may hold values from 0.0005 to 0.002
- mean_feature: float32 [32, 256, 768], P('cell'), may hold values from -2 to 2
- square_feature: float32 [32, 256, 768], P('cell'), may hold values from 0.0005 to 0.002
- target_color: bfloat16 [4096, 768], P('rays'), may hold values from -6 to 6
Outputs:
- rendered: bfloat16 [4096, 768], P('rays', 'cell')
- depth_grad: float32 [4096, 32], P('rays', 'cell')
- update_second: bfloat16 [32, 256, 256], P('cell')
- update_feature: bfloat16 [32, 256, 768], P('cell')
Inputs may be any that keep to these rules, and one draw needn't show every extreme that they name: Samples of a ray in a cell use the table rows entry_index to entry_index + 7. Slots from sample_count on lie outside the cell.
All inputs are finite; a program needn't handle non-finite values.
Results may differ from a plain program's by a relative error of at most 0.0075.
Values may be sent and summed in bfloat16 or wider, within the bound.
A program may use at most 64 MiB of HBM per device.

v0:
```python
import jax
import jax.numpy as jnp
from jax import lax
from jax.sharding import Mesh
from jax.sharding import PartitionSpec as P

SAMPLES = 8
CELL = ("cell_0", "cell_1")
RAYS = ("rays_0", "rays_1")
CELL_RAYS = ("cell_0", "cell_1", "rays_0", "rays_1")


beta_first = 0.9
beta_second = 0.999
bias_first = 0.19
bias_second = 0.001999
adam_floor = 1e-08
mean_floor = 1e-06


def sent_to_all(array, axis):
    copies = jnp.broadcast_to(array, (lax.axis_size(axis), *array.shape))
    return lax.all_to_all(copies, axis, split_axis=0, concat_axis=0, tiled=True)


def joined_by_halves(pieces, combine):
    while len(jax.tree.leaves(pieces)[0]) > 1:
        pieces = jax.vmap(combine)(*(pieces[side::2] for side in (0, 1)))
    return pieces[0]


def entering(array, axis, combine, identity, reverse):
    length, position = (lax.axis_size(axis), lax.axis_index(axis))
    passed = jnp.arange(length) > position if reverse else jnp.arange(length) < position

    def kept(part, zero, own):
        part = jnp.where(
            passed.reshape(-1, *(1 for _ in own.shape)), part, jnp.asarray(zero, own.dtype)
        )
        return part[::-1] if reverse else part

    pieces = sent_to_all(array, axis)
    return joined_by_halves(kept(pieces, identity, array), combine)


def cut_along(array, dim, length):
    before, after = (array.shape[:dim], array.shape[dim + 1 :])
    return jnp.moveaxis(array.reshape(*before, length, -1, *after), dim, 0)


def sum_at_owner(array, axis, dim):
    blocks = cut_along(array, dim, lax.axis_size(axis))
    arrived = lax.all_to_all(blocks, axis, split_axis=0, concat_axis=0, tiled=True)
    return arrived.sum(axis=0)


def joined_along(blocks, dim):
    blocks = jnp.moveaxis(blocks, 0, dim)
    lengths = blocks.shape
    return blocks.reshape(*lengths[:dim], lengths[dim] * lengths[dim + 1], *lengths[dim + 2 :])


def stacked_from(array, axes, turns):
    blocks = array
    for k in turns:
        blocks = lax.all_gather(blocks, axes[k])
    done = turns[::-1]
    back = [done.index(k) for k in range(len(axes))]
    blocks = blocks.transpose(*back, *range(len(axes), blocks.ndim))
    return blocks.reshape(-1, *array.shape)


def whole_of(array, axes, turns, dim):
    return joined_along(stacked_from(array, axes, turns), dim)


def side_by_side(arrays, axis, dim, along):
    ends, at = ([], 0)
    for a in arrays[:-1]:
        at += a.shape[along]
        ends.append(at)
    both = jnp.concatenate(arrays, axis=along)
    return tuple(jnp.split(sum_at_owner(both, axis, dim), ends, axis=along))


def by_axis(array, axes):
    for axis in axes:
        array = lax.psum(array, axis)
    return array


def side_by_side_2(arrays, axis, dim, along):
    ends, at = ([], 0)
    for a in arrays[:-1]:
        at += a.shape[along]
        ends.append(at)
    both = jnp.concatenate(arrays, axis=along)
    return tuple(jnp.split(lax.all_gather(both, axis, axis=dim, tiled=True), ends, axis=along))


def cell_forward(
    ray_feat,
    place_table,
    entry_index,
    sample_count,
    step_length,
    w_first,
    w_second,
    w_density,
    w_feature,
):
    ray_rows = ray_feat.shape[0]
    offsets = jnp.arange(SAMPLES, dtype=jnp.int32)
    sample_spot = entry_index[:, None] + offsets[None, :]
    table_slot = jnp.arange(place_table.shape[0], dtype=jnp.int32)
    one_hot = (sample_spot.reshape(-1, 1) == table_slot[None, :]).astype(jnp.bfloat16)
    placed = jnp.dot(one_hot, place_table, preferred_element_type=jnp.float32)
    inputs = (
        placed.reshape(ray_rows, SAMPLES, -1) + ray_feat[:, None, :].astype(jnp.float32)
    ).astype(jnp.bfloat16)
    inputs = inputs.reshape(ray_rows * SAMPLES, -1)
    hidden_one = jax.nn.relu(jnp.dot(inputs, w_first, preferred_element_type=jnp.float32)).astype(
        jnp.bfloat16
    )
    before = jnp.dot(hidden_one, w_second.astype(jnp.bfloat16), preferred_element_type=jnp.float32)
    hidden_two = jax.nn.relu(before).astype(jnp.bfloat16)
    feature = jnp.dot(
        hidden_two, w_feature.astype(jnp.bfloat16), preferred_element_type=jnp.float32
    )
    density_logit = jnp.dot(hidden_two, w_density, preferred_element_type=jnp.float32)
    inside = (offsets[None, :] < sample_count[:, None]).astype(jnp.float32)
    travel = step_length[:, None] * inside
    depth_step = jax.nn.softplus(density_logit).reshape(ray_rows, SAMPLES) * travel
    return (hidden_one, before, hidden_two, feature, density_logit, travel, depth_step)


def composite(depth_step, feature_cube):
    ahead_depth = jnp.cumsum(depth_step, axis=1) - depth_step
    weight = jnp.exp(-ahead_depth) * (1.0 - jnp.exp(-depth_step))
    partial_value = jnp.einsum("rs,rsf->rf", weight, feature_cube)
    return (partial_value, jnp.sum(depth_step, axis=1))


def cell_backward(stored, w_density, w_feature, grad_part, grad_depth):
    hidden_one, before, hidden_two, feature, density_logit, travel, depth_step = stored
    ray_rows = depth_step.shape[0]
    feature_cube = feature.reshape(ray_rows, SAMPLES, -1)
    _, pullback = jax.vjp(composite, depth_step, feature_cube)
    grad_step, grad_cube = pullback((grad_part, grad_depth))
    grad_rows = grad_cube.reshape(ray_rows * SAMPLES, -1).astype(jnp.bfloat16)
    grad_feature = jnp.dot(hidden_two.T, grad_rows, preferred_element_type=jnp.float32)
    grad_logit = (grad_step * travel).reshape(-1) * jax.nn.sigmoid(density_logit)
    grad_hidden = jnp.dot(
        grad_rows, w_feature.astype(jnp.bfloat16).T, preferred_element_type=jnp.float32
    )
    grad_hidden = grad_hidden + grad_logit[:, None] * w_density.astype(jnp.float32)[None, :]
    grad_before = jnp.where(before > 0, grad_hidden, 0.0).astype(jnp.bfloat16)
    grad_second = jnp.dot(hidden_one.T, grad_before, preferred_element_type=jnp.float32)
    return (grad_second, grad_feature)


def adam_update(gradient, mean_moment, square_moment, rescale):
    unit_grad = gradient * rescale
    mean_new = beta_first * mean_moment + (1.0 - beta_first) * unit_grad
    square_new = beta_second * square_moment + (1.0 - beta_second) * unit_grad * unit_grad
    return (mean_new / bias_first / (jnp.sqrt(square_new / bias_second) + adam_floor)).astype(
        jnp.bfloat16
    )


def combine_sum(earlier, later_part):
    return earlier + later_part


def on_device(
    ray_code,
    entry_index,
    sample_count,
    step_length,
    positions,
    w_first,
    w_second,
    w_density,
    w_feature,
    mean_second,
    square_second,
    mean_feature,
    square_feature,
    target_color,
):
    ray_rows = ray_code.shape[0]
    stored = cell_forward(
        ray_code[:, 0, :],
        positions[0],
        entry_index[:, 0],
        sample_count[:, 0],
        step_length[:, 0],
        w_first[0],
        w_second[0],
        w_density[0],
        w_feature[0],
    )
    feature_cube = stored[3].reshape(ray_rows, SAMPLES, -1)
    partial_value, depths = composite(stored[6], feature_cube)
    cell_place = lax.axis_index(CELL)
    cell_total = lax.axis_size(CELL)
    ahead_depth = entering(depths, CELL, combine_sum, jnp.zeros_like(depths), False)
    transmit = jnp.exp(-ahead_depth)
    lit_part = transmit[:, None] * partial_value
    column_width = partial_value.shape[1] // cell_total
    column_start = cell_place * column_width
    share_sum = sum_at_owner(lit_part, CELL, 1)
    rendered = share_sum.astype(jnp.bfloat16)
    own_target = lax.dynamic_slice_in_dim(target_color, column_start, column_width, 1).astype(
        jnp.float32
    )
    residual = whole_of(share_sum - own_target, CELL, (0, 1), 1)
    grad_part = transmit[:, None] * residual
    bright = transmit * jnp.sum(partial_value * residual, axis=1)
    later_sum = entering(bright, CELL, combine_sum, jnp.zeros_like(bright), True)
    depth_grad = -later_sum[:, None]
    grad_second, grad_feature = cell_backward(
        stored, w_density[0], w_feature[0], grad_part, -later_sum
    )
    entry_total = cell_total * (grad_second.size + grad_feature.size)
    share_second, share_feature = side_by_side((grad_second, grad_feature), RAYS, 0, 1)
    share_rows = share_second.shape[0]
    row_start = lax.axis_index(RAYS) * share_rows
    local_square = jnp.sum(share_second * share_second) + jnp.sum(share_feature * share_feature)
    square_sum = by_axis(local_square, CELL_RAYS)
    rescale = lax.rsqrt(square_sum / entry_total + mean_floor)
    piece_second = adam_update(
        share_second,
        lax.dynamic_slice_in_dim(mean_second[0], row_start, share_rows, 0),
        lax.dynamic_slice_in_dim(square_second[0], row_start, share_rows, 0),
        rescale,
    )
    piece_feature = adam_update(
        share_feature,
        lax.dynamic_slice_in_dim(mean_feature[0], row_start, share_rows, 0),
        lax.dynamic_slice_in_dim(square_feature[0], row_start, share_rows, 0),
        rescale,
    )
    update_second, update_feature = side_by_side_2((piece_second, piece_feature), RAYS, 0, 1)
    return (rendered, depth_grad, update_second[None], update_feature[None])


def solution(mesh):
    split = Mesh(mesh.devices.reshape(16, 2, 4, 4), ("cell_0", "cell_1", "rays_0", "rays_1"))
    return jax.shard_map(
        on_device,
        mesh=split,
        in_specs=(
            P(RAYS, CELL, None),
            P(RAYS, CELL),
            P(RAYS, CELL),
            P(RAYS, CELL),
            P(CELL, None, None),
            P(CELL, None, None),
            P(CELL, None, None),
            P(CELL, None),
            P(CELL, None, None),
            P(CELL, None, None),
            P(CELL, None, None),
            P(CELL, None, None),
            P(CELL, None, None),
            P(RAYS, None),
        ),
        out_specs=(P(RAYS, CELL), P(RAYS, CELL), P(CELL, None, None), P(CELL, None, None)),
        check_vma=False,
    )
```

profile of v0, /device:TPU:8, one launch (start us, length us, event | category | flops | bytes accessed | tf_op | source)
XLA Modules:
  0.0 281.2 jit_solution(15000017610222860366)
XLA Ops:
  8.2 15.6 %all-to-all-start = ((f32[32,1,256]{2,1,0:T(1,128)}), f32[32,1,256]{2,1,0:T(1,128)}, u32[]{:S(2)}, u32[]{:S(2)}) async-start(f32[32,1,256]{2,1,0:T(1,128)} %broadcast_in_dim.43), calls=%async_computation | async-start | bytes 65536 | tf_op jit(solution)/shard_map/all_to_all | solution.py:23
  24.0 1.8 reduce_window_sum.24
  26.8 2.3 fusion.27
  30.7 3.0 %fusion.2 = f32[256,1,768]{2,1,0:T(1,128)} fusion(f32[256,8,1]{1,2,0:T(1,128)S(1)} %bitcast.121, bf16[256,8,768]{2,0,1:T(8,128)(2,1)S(1)} %fusion.27), kind=kOutput, calls=%fused_computation.3 | convolution fusion | flops 3145728 | bytes 3940352 | tf_op jit(solution)/shard_map/rs,rsf->rf/dot_general | solution.py:140
  33.7 2.2 copy.48
  38.8 11.4 %all-to-all-start.1 = ((f32[32,256,24]{1,2,0:T(8,128)}), f32[32,256,24]{1,2,0:T(8,128)}, u32[]{:S(2)}, u32[]{:S(2)}) async-start(f32[32,256,24]{1,2,0:T(8,128)} %bitcast.118), calls=%async_computation.1 | async-start | bytes 1572864 | tf_op jit(solution)/shard_map/all_to_all | solution.py:53
  51.0 44.1 %all-to-all-done.1 = f32[32,256,24]{1,2,0:T(8,128)} async-done(((f32[32,256,24]{1,2,0:T(8,128)}), f32[32,256,24]{1,2,0:T(8,128)}, u32[]{:S(2)}, u32[]{:S(2)}) %all-to-all-start.1) | async-done | bytes 786464 | tf_op jit(solution)/shard_map/all_to_all | solution.py:53
  96.9 28.5 %all-gather = f32[4096,24]{0,1:T(8,128)S(1)} all-gather(f32[256,24]{0,1:T(8,128)S(1)} %get-tuple-element.8), channel_id=2, replica_groups=mesh['cell_0'=16,'cell_1'=2,'rays_0'=4,'rays_1'=4] {'cell_0'}, dimensions={0}, use_global_device_ids=true | all-gather | bytes 417792 | tf_op jit(solution)/shard_map/all_gather | solution.py:66
  125.6 2.4 all-gather.1
  129.8 2.0 copy.49
  131.8 5.3 %fusion = f32[256,1,8]{2,1,0:T(1,128)} fusion(bf16[256,768,1]{1,2,0:T(2,128)(2,1)} %copy.49, bf16[256,8,768]{2,0,1:T(8,128)(2,1)} %copy-done.1), kind=kOutput, calls=%fused_computation.1 | convolution fusion | flops 3145728 | bytes 3547136 | tf_op jit(solution)/shard_map/transpose(jvp(rs,rsf->rf))/dot_general | solution.py:140
  137.7 5.1 %all-to-all-start.2 = ((f32[32,1,256]{2,1,0:T(1,128)}), f32[32,1,256]{2,1,0:T(1,128)}, u32[]{:S(2)}, u32[]{:S(2)}) async-start(f32[32,1,256]{2,1,0:T(1,128)} %broadcast_in_dim.46), calls=%async_computation.2 | async-start | bytes 65536 | tf_op jit(solution)/shard_map/all_to_all | solution.py:23
  142.8 3.3 %fusion.5 = f32[256,768]{1,0:T(8,128)} fusion(f32[256,768]{1,0:T(8,128)} %copy.44, f32[256,8]{1,0:T(8,128)} %copy-done.8, f32[2048,256]{1,0:T(8,128)S(1)} %fusion.43), kind=kOutput, calls=%fused_computation.6 | convolution fusion | flops 809500672 | bytes 3678208 | tf_op jit(solution)/shard_map/dot_general | solution.py:151
  148.6 7.0 %all-to-all-done.2 = f32[32,1,256]{2,1,0:T(1,128)} async-done(((f32[32,1,256]{2,1,0:T(1,128)}), f32[32,1,256]{2,1,0:T(1,128)}, u32[]{:S(2)}, u32[]{:S(2)}) %all-to-all-start.2) | async-done | bytes 32800 | tf_op jit(solution)/shard_map/all_to_all | solution.py:23
  170.2 1.8 select_multiply_fusion
  173.7 3.0 %fusion.24 = f32[256,256]{1,0:T(8,128)S(1)} fusion(bf16[2048,256]{1,0:T(8,128)(2,1)} %copy-done.6, f32[256,768]{1,0:T(8,128)} %copy.44, f32[256,8]{1,0:T(8,128)} %copy-done.8, f32[2048,256]{1,0:T(8,128)S(1)} %fusion.43, f32[256]{0:T(256)} %mul.193, f32[2048]{0:T(1024)} %divide_multiply_fusion, f32[1,256,768]{2,1,0:T(8,128)S(1)} %copy-done.7), kind=kOutput, calls=%fused_computation.19 | convolution fusion | flops 1079705600 | bytes 4998144 | tf_op jit(solution)/shard_map/dot_general | solution.py:158
  176.6 2.2 pad_maximum_fusion
  178.9 7.4 %all-to-all-start.3 = ((f32[16,16,1024]{2,1,0:T(8,128)}), f32[16,16,1024]{2,1,0:T(8,128)S(1)}, u32[]{:S(2)}, u32[]{:S(2)}) async-start(f32[16,16,1024]{2,1,0:T(8,128)} %bitcast.35), calls=%async_computation.3 | async-start | bytes 2097152 | tf_op jit(solution)/shard_map/all_to_all | solution.py:53
  186.3 14.1 %all-to-all-done.3 = f32[16,16,1024]{2,1,0:T(8,128)S(1)} async-done(((f32[16,16,1024]{2,1,0:T(8,128)}), f32[16,16,1024]{2,1,0:T(8,128)S(1)}, u32[]{:S(2)}, u32[]{:S(2)}) %all-to-all-start.3) | async-done | bytes 1048608 | tf_op jit(solution)/shard_map/all_to_all | solution.py:53
  202.9 28.2 %psum.28 = f32[]{:T(128)} all-reduce(f32[]{:T(128)S(6)} %add.155), channel_id=1, replica_groups=mesh['cell_0'=16,'cell_1'=2,'rays_0'=4,'rays_1'=4] {'cell_0'}, use_global_device_ids=true, to_apply=%region_8.9 | all-reduce | flops 1 | bytes 8 | tf_op jit(solution)/shard_map/psum | solution.py:88
  231.1 3.1 %psum.29 = f32[]{:T(128)} all-reduce(f32[]{:T(128)} %psum.28), channel_id=1, replica_groups=mesh['cell_0'=16,'cell_1'=2,'rays_0'=4,'rays_1'=4] {'cell_1'}, use_global_device_ids=true, to_apply=%region_9.10 | all-reduce | flops 1 | bytes 8 | tf_op jit(solution)/shard_map/psum | solution.py:88
  234.2 11.4 %psum.30 = f32[]{:T(128)} all-reduce(f32[]{:T(128)} %psum.29), channel_id=1, replica_groups=mesh['cell_0'=16,'cell_1'=2,'rays_0'=4,'rays_1'=4] {'rays_0'}, use_global_device_ids=true, to_apply=%region_10.11 | all-reduce | flops 1 | bytes 8 | tf_op jit(solution)/shard_map/psum | solution.py:88
  246.1 8.5 %psum.31 = f32[]{:T(128)} all-reduce(f32[]{:T(128)} %psum.30), channel_id=1, replica_groups=mesh['cell_0'=16,'cell_1'=2,'rays_0'=4,'rays_1'=4] {'rays_1'}, use_global_device_ids=true, to_apply=%region_11.12 | all-reduce | flops 1 | bytes 8 | tf_op jit(solution)/shard_map/psum | solution.py:88
  257.0 22.7 %all_gather.19 = bf16[256,1024]{1,0:T(8,128)(2,1)S(1)} all-gather(bf16[16,1024]{1,0:T(8,128)(2,1)S(1)} %pad_maximum_fusion.1), channel_id=1, replica_groups=mesh['cell_0'=16,'cell_1'=2,'rays_0'=4,'rays_1'=4] {'rays_0','rays_1'}, dimensions={0}, use_global_device_ids=true | all-gather | bytes 557056 | tf_op jit(solution)/shard_map/all_gather | solution.py:98
  (99 shorter events, 42.0 us)
Async XLA Ops:
  0.6 49.6 %copy-start = (bf16[256,768]{1,0:T(8,128)(2,1)S(1)}, bf16[256,768]{1,0:T(8,128)(2,1)}, u32[]{:S(2)}) copy-start(bf16[256,768]{1,0:T(8,128)(2,1)} %param.27) | copy-start | bytes 1179652
  0.6 4.9 %copy-start.10 = (f32[1,256,256]{2,1,0:T(8,128)S(1)}, f32[1,256,256]{2,1,0:T(8,128)}, u32[]{:S(2)}) copy-start(f32[1,256,256]{2,1,0:T(8,128)} %param.20) | copy-start | bytes 786436
  5.6 1.1 copy-start.6
  5.6 0.7 copy-start.13
  5.6 1.2 copy-start.11
  5.6 1.2 copy-start.12
  8.2 28.6 %all-to-all-start = ((f32[32,1,256]{2,1,0:T(1,128)}), f32[32,1,256]{2,1,0:T(1,128)}, u32[]{:S(2)}, u32[]{:S(2)}) async-start(f32[32,1,256]{2,1,0:T(1,128)} %broadcast_in_dim.43), calls=%async_computation | async-start | bytes 65536 | tf_op jit(solution)/shard_map/all_to_all | solution.py:23
  26.8 2.3 copy-start.8
  29.1 1.7 copy-start.1
  35.9 60.4 %copy-start.2 = (f32[256,1,768]{0,2,1:T(8,128)}, f32[256,1,768]{0,2,1:T(8,128)S(1)}, u32[]{:S(2)}) copy-start(f32[256,1,768]{0,2,1:T(8,128)S(1)} %copy.48) | copy-start | bytes 2359300
  38.8 56.3 %all-to-all-start.1 = ((f32[32,256,24]{1,2,0:T(8,128)}), f32[32,256,24]{1,2,0:T(8,128)}, u32[]{:S(2)}, u32[]{:S(2)}) async-start(f32[32,256,24]{1,2,0:T(8,128)} %bitcast.118), calls=%async_computation.1 | async-start | bytes 1572864 | tf_op jit(solution)/shard_map/all_to_all | solution.py:53
  96.9 31.5 %copy-start.3 = (f32[256,1,768]{0,2,1:T(8,128)S(1)}, f32[256,1,768]{0,2,1:T(8,128)}, u32[]{:S(2)}) copy-start(f32[256,1,768]{0,2,1:T(8,128)} %copy-done.2) | copy-start | bytes 2359300
  137.7 17.9 %all-to-all-start.2 = ((f32[32,1,256]{2,1,0:T(1,128)}), f32[32,1,256]{2,1,0:T(1,128)}, u32[]{:S(2)}, u32[]{:S(2)}) async-start(f32[32,1,256]{2,1,0:T(1,128)} %broadcast_in_dim.46), calls=%async_computation.2 | async-start | bytes 65536 | tf_op jit(solution)/shard_map/all_to_all | solution.py:23
  142.8 3.3 %copy-start.4 = (f32[256,8]{1,0:T(8,128)S(1)}, f32[256,8]{1,0:T(8,128)}, u32[]{:S(2)}) copy-start(f32[256,8]{1,0:T(8,128)} %get-tuple-element.5) | copy-start | bytes 24580
  142.8 3.3 %copy-start.5 = (f32[256,8]{1,0:T(8,128)S(1)}, f32[256,8]{1,0:T(8,128)}, u32[]{:S(2)}) copy-start(f32[256,8]{1,0:T(8,128)} %reduce_window_sum.24) | copy-start | bytes 24580
  142.8 3.3 %copy-start.9 = (f32[256,1,8]{2,1,0:T(1,128)S(1)}, f32[256,1,8]{2,1,0:T(1,128)}, u32[]{:S(2)}) copy-start(f32[256,1,8]{2,1,0:T(1,128)} %fusion) | copy-start | bytes 24580
  142.8 30.9 %copy-start.7 = (f32[1,256,768]{2,1,0:T(8,128)S(1)}, f32[1,256,768]{2,1,0:T(8,128)}, u32[]{:S(2)}) copy-start(f32[1,256,768]{2,1,0:T(8,128)} %param.22) | copy-start | bytes 2359300
  178.9 21.5 %all-to-all-start.3 = ((f32[16,16,1024]{2,1,0:T(8,128)}), f32[16,16,1024]{2,1,0:T(8,128)S(1)}, u32[]{:S(2)}, u32[]{:S(2)}) async-start(f32[16,16,1024]{2,1,0:T(8,128)} %bitcast.35), calls=%async_computation.3 | async-start | bytes 2097152 | tf_op jit(solution)/shard_map/all_to_all | solution.py:53
where the time goes:
time: 283 us; the launch traced here: 281 us
  blocking collectives  105 us (37%)
  waiting for transfers between devices  66.1 us (23%)
  starting transfers between devices  39.5 us (14%)
  other arithmetic  25.3 us (9%)
  local copies, waits for them, and re-layouts  21.8 us (8%)
  matrix products  20.8 us (7%)
  between operations  2.96 us (1%)
    all_to_all x2, waiting for transfers between devices, sum_at_owner(): lax.all_to_all(blocks, axis, split_axis=0, concat_axis=0, tiled=True)  58.2 us
    psum x4, blocking collectives, by_axis(): array = lax.psum(array, axis)  51.1 us
    all_gather x2, blocking collectives, stacked_from(): blocks = lax.all_gather(blocks, axes[k])  30.9 us
    all_gather x1, blocking collectives, side_by_side_2(): lax.all_gather(both, axis, axis=dim, tiled=True)  22.7 us
    all_to_all x2, starting transfers between devices, sent_to_all(): return lax.all_to_all(copies, axis, split_axis=0, concat_axis=0, tiled=True)  20.7 us
    all_to_all x2, starting transfers between devices, sum_at_owner(): lax.all_to_all(blocks, axis, split_axis=0, concat_axis=0, tiled=True)  18.8 us
    slice x18, local copies, waits for them, and re-layouts, joined_by_halves(): pieces = jax.vmap(combine)(*(pieces[side::2] for side in (0, 1)))  9.95 us
    dot_general x2, matrix products, composite(): partial_value = jnp.einsum('rs,rsf->rf', weight, feature_cube)  8.29 us
  transfers between devices with their start and end apart: 4, of which 4 were waited for; matrix products, arithmetic and copies ran while one was open for 6% of the time, Pallas kernels for 0%

commit v1 on v0

v1 whole, which is shorter than its diff:
```python
import functools

import jax
import jax.numpy as jnp
from jax import lax
from jax.experimental import pallas as pl
from jax.experimental.pallas import tpu as pltpu
from jax.sharding import Mesh
from jax.sharding import PartitionSpec as P

SAMPLES = 8
MESH = pl.DeviceIdType.MESH
CELL = ("z", "core")
RAYS = ("y", "x")
HALF = 128
F32 = jnp.float32
BF16 = jnp.bfloat16

beta_first = 0.9
beta_second = 0.999
bias_first = 0.19
bias_second = 0.001999
adam_floor = 1e-08
mean_floor = 1e-06


def nt_dot(a, b):
    return lax.dot_general(a, b, (((1,), (1,)), ((), ())), preferred_element_type=F32)


def mm(a, b):
    return jnp.dot(a, b, preferred_element_type=F32)


def kernel(
    sizes,
    ray_h, ent_h, cnt_h, stp_h, pos_h, w1_h, w2_h, wd_h, wf_h,
    ms_h, vs_h, mf_h, vf_h, tgt_h,
    ren_o, dg_o, us_o, uf_o,
    ray_v, ent_v, cnt_v, stp_v, pos_v, w1_v, w2_v, wd_v, wf_v,
    ms_v, vs_v, mf_v, vf_v, tgt_v,
    rayt, post, w1t, w2t, wft, wfb, wdb, h1, h2, lg, tgt_t, q_t, gp,
    dep, tt, pl_s, pr_s, ns_s, nr_s, fs_s, fr_s, cp_s, cr_s, rs_s, br,
    gf_s, gf_r, gs_s, gs_r, ga, sq, sr,
    loc, many_send, many_recv, one_send, one_recv,
):
    n_z, n_y, n_x, all_cells = sizes
    n_cell, n_rays = 2 * n_z, n_y * n_x
    z, core = lax.axis_index("z"), lax.axis_index("core")
    y, x = lax.axis_index("y"), lax.axis_index("x")
    cell = 2 * z + core
    group = n_x * y + x
    quad, res = lax.div(z, 4), lax.rem(z, 4)
    other = 1 - core

    def cell_device(t):
        return (lax.div(t, 2), lax.rem(t, 2), y, x)

    def rays_device(t):
        return (z, core, lax.div(t, n_x), lax.rem(t, n_x))

    def chip_device(t):
        return (lax.rem(t + n_z, n_z), core, y, x)

    sibling = (z, other, y, x)

    def each_cell(send):
        lax.fori_loop(1, n_cell, lambda j, n: (send(lax.rem(cell + j, n_cell)), n)[1], 0)

    def each_group(send):
        def step(j, n):
            to_y = lax.rem(y + lax.div(j, n_x), n_y)
            to_x = lax.rem(x + lax.rem(j, n_x), n_x)
            send(to_y * n_x + to_x)
            return n

        lax.fori_loop(1, n_rays, step, 0)

    bring = {}
    for i, (name, src, dst) in enumerate((
        ("ent", ent_h, ent_v), ("pos", pos_h, pos_v), ("ray", ray_h, ray_v), ("w1", w1_h, w1_v),
        ("w2", w2_h, w2_v), ("wd", wd_h, wd_v), ("cnt", cnt_h, cnt_v), ("stp", stp_h, stp_v),
        ("wf", wf_h, wf_v),
        ("tgt", tgt_h.at[pl.ds(pl.multiple_of(core * HALF, HALF), HALF), :], tgt_v),
        ("ms", ms_h, ms_v), ("vs", vs_h, vs_v), ("mf", mf_h, mf_v), ("vf", vf_h, vf_v),
    )):
        bring[name] = pltpu.make_async_copy(src, dst, loc.at[i])
        bring[name].start()

    barrier = pltpu.get_barrier_semaphore()
    each_cell(lambda t: pl.semaphore_signal(barrier, inc=1, device_id=cell_device(t), device_id_type=MESH))
    each_group(lambda t: pl.semaphore_signal(barrier, inc=1, device_id=rays_device(t), device_id_type=MESH))

    for name in ("ent", "pos", "ray", "w1"):
        bring[name].wait()
    post[...] = pos_v[...].astype(F32).T.astype(BF16)
    rayt[...] = ray_v[...].astype(F32).T
    w1t[...] = w1_v[...].astype(F32).T.astype(BF16)
    for name in ("w2", "wd", "cnt", "stp"):
        bring[name].wait()
    w2t[...] = w2_v[...].T.astype(BF16)
    width = wd_v.shape[1]
    n_rows = ray_v.shape[0]
    wdb[...] = jnp.broadcast_to(wd_v[...].astype(F32), (n_rows, width)).T
    slot = lax.broadcasted_iota(jnp.int32, (pos_v.shape[0], n_rows), 0)

    def forward(k):
        hot = jnp.where(slot == ent_v[...] + k, 1.0, 0.0).astype(BF16)
        inputs = (mm(post[...], hot) + rayt[...]).astype(BF16)
        first = jnp.maximum(mm(w1t[...], inputs), 0.0).astype(BF16)
        second = jnp.maximum(mm(w2t[...], first), 0.0).astype(BF16)
        h1[k] = first
        h2[k] = second
        lg[pl.ds(k, 1), :] = jnp.sum(second.astype(F32) * wdb[...], axis=0, keepdims=True)

    def two(i, n):
        forward(2 * i)
        forward(2 * i + 1)
        return n

    lax.fori_loop(0, SAMPLES // 2, two, 0)

    order = lax.broadcasted_iota(jnp.int32, (SAMPLES, n_rows), 0)
    logit = lg[...]
    travel = jnp.where(order < cnt_v[...], stp_v[...], 0.0)
    step_depth = (jnp.maximum(logit, 0.0) + jnp.log1p(jnp.exp(-jnp.abs(logit)))) * travel

    def ahead_of(v):
        total = v
        for shift in (1, 2, 4):
            total = total + jnp.where(order >= shift, pltpu.roll(total, shift, 0), 0.0)
        return total - v

    ahead = jnp.exp(-ahead_of(step_depth))
    kept = jnp.exp(-step_depth)
    weight = ahead * (1.0 - kept)
    depth = jnp.sum(step_depth, axis=0, keepdims=True)

    def put_rows(buf, at, row):
        for half in range(2):
            buf[at, pl.ds(half, 1), :] = row[:, half * HALF:(half + 1) * HALF]

    put_rows(dep, cell, depth)
    pl.semaphore_wait(barrier, n_cell - 1 + n_rays - 1)

    def to_cells(buf, i):
        each_cell(lambda t: pltpu.make_async_remote_copy(
            buf.at[cell], buf.at[cell], many_send.at[i], many_recv.at[i],
            device_id=cell_device(t), device_id_type=MESH).start())

    def to_groups(src, dst, i):
        each_group(lambda t: pltpu.make_async_remote_copy(
            src(t), dst.at[group], many_send.at[i], many_recv.at[i],
            device_id=rays_device(t), device_id_type=MESH).start())

    def wait_many(buf, sem, i):
        part = buf.at[pl.ds(0, buf.shape[0] - 1)]
        pltpu.make_async_copy(part, part, sem.at[i]).wait()

    sent = []

    def send(src, dst, i, device):
        copy = pltpu.make_async_remote_copy(
            src, dst, one_send.at[i], one_recv.at[i], device_id=device, device_id_type=MESH)
        copy.start()
        sent.append(copy)

    def arrived(dst, i):
        pltpu.make_async_copy(dst, dst, one_recv.at[i]).wait()

    to_cells(dep, 0)

    gather = weight[0:1] * h2[0].astype(F32)
    for k in range(1, SAMPLES):
        gather = gather + weight[k:k + 1] * h2[k].astype(F32)
    gathered = gather.astype(BF16)
    bring["wf"].wait()
    wfb[...] = wf_v[...].astype(BF16)
    wft[...] = wf_v[...].T.astype(BF16)
    partial = mm(wft[...], gathered).astype(BF16)
    for half in range(2):
        pl_s[half] = partial[:, half * HALF:(half + 1) * HALF].reshape(pl_s.shape[1:])
    send(pl_s.at[other], pr_s, 0, sibling)
    bring["tgt"].wait()
    tgt_t[...] = tgt_v[...].astype(F32).T.reshape(tgt_t.shape)

    wait_many(dep, many_recv, 0)
    number = lax.broadcasted_iota(jnp.int32, dep.shape, 0)
    depths = dep[...]
    before_pair = jnp.sum(jnp.where(number < 2 * z, depths, 0.0), axis=0)
    tt[0] = jnp.exp(-before_pair)
    tt[1] = jnp.exp(-(before_pair + dep[2 * z]))
    mine = tt[core, pl.ds(core, 1), :]
    theirs = tt[other, pl.ds(core, 1), :]

    arrived(pr_s, 0)
    for i in range(16):
        ns_s[i // 4, i % 4] = (mine * pl_s[core, i].astype(F32) + theirs * pr_s[i].astype(F32)).astype(BF16)

    def turn(a):
        return lax.rem(res + a + 4, 4)

    send(ns_s.at[:, turn(1)], nr_s.at[0], 1, chip_device(z + 1))
    send(ns_s.at[:, turn(-1)], nr_s.at[1], 2, chip_device(z - 1))
    send(ns_s.at[pl.ds(0, 2), turn(2)], nr_s.at[2, pl.ds(0, 2)], 3, chip_device(z + 2))
    send(ns_s.at[pl.ds(2, 2), turn(2)], nr_s.at[2, pl.ds(2, 2)], 4, chip_device(z - 2))
    arrived(nr_s.at[0], 1)
    arrived(nr_s.at[1], 2)
    arrived(nr_s.at[2, pl.ds(0, 2)], 3)
    arrived(nr_s.at[2, pl.ds(2, 2)], 4)
    for i in range(4):
        fs_s[i] = (
            ns_s[i, res].astype(F32) + nr_s[0, i].astype(F32)
            + nr_s[1, i].astype(F32) + nr_s[2, i].astype(F32)
        ).astype(BF16)
    for i in range(1, 4):
        to = lax.rem(quad + i, 4)
        send(fs_s.at[to], fr_s.at[i - 1], 4 + i, chip_device(4 * to + res))
    for i in range(1, 4):
        arrived(fr_s.at[i - 1], 4 + i)
    lit = fs_s[quad].astype(F32)
    for i in range(3):
        lit = lit + fr_s[i].astype(F32)

    rs_s[core, quad, res] = (lit - tgt_t[z]).astype(BF16)
    for i in range(1, 4):
        send(rs_s.at[core, quad, res], rs_s.at[core, quad, res], 7 + i,
             chip_device(4 * lax.rem(quad + i, 4) + res))
    cp_s[...] = lit.reshape(cp_s.shape)
    send(cp_s.at[other], cr_s, 11, sibling)
    for i in range(1, 4):
        arrived(rs_s.at[core, lax.rem(quad - i + 4, 4), res], 7 + i)
    own = rs_s.at[core, :, res]
    low, high = rs_s.at[core, pl.ds(0, 2), res], rs_s.at[core, pl.ds(2, 2), res]
    send(own, own, 12, chip_device(z + 1))
    send(own, own, 13, chip_device(z - 1))
    send(low, low, 14, chip_device(z + 2))
    send(high, high, 15, chip_device(z - 2))
    send(own, own, 16, sibling)
    came = (
        rs_s.at[core, :, turn(-1)], rs_s.at[core, :, turn(1)],
        rs_s.at[core, pl.ds(0, 2), turn(2)], rs_s.at[core, pl.ds(2, 2), turn(2)],
    )
    for i, block in enumerate(came):
        arrived(block, 12 + i)
        send(block, block, 17 + i, sibling)
    arrived(rs_s.at[other, :, res], 16)
    for i, block in enumerate((
        rs_s.at[other, :, turn(-1)], rs_s.at[other, :, turn(1)],
        rs_s.at[other, pl.ds(0, 2), turn(2)], rs_s.at[other, pl.ds(2, 2), turn(2)],
    )):
        arrived(block, 17 + i)

    transmit = tt[core]
    for half in range(2):
        block = rs_s[half].reshape(gp.shape[0], HALF).astype(F32)
        gp[:, half * HALF:(half + 1) * HALF] = (block * transmit[half:half + 1]).astype(BF16)
    q_t[...] = mm(wfb[...], gp[...])
    slopes = []
    for k in range(SAMPLES):
        slopes.append(jnp.sum(h2[k].astype(F32) * q_t[...], axis=0, keepdims=True))
    slope = jnp.concatenate(slopes, axis=0)
    lit_slope = weight * slope
    put_rows(br, cell, jnp.sum(lit_slope, axis=0, keepdims=True))
    to_cells(br, 1)
    gf_s[...] = nt_dot(gathered, gp[...]).astype(BF16).reshape(gf_s.shape)
    to_groups(lambda t: gf_s.at[t], gf_r, 2)

    arrived(cr_s, 11)
    first_half = jnp.where(core == 0, cp_s[core], cr_s[...])
    second_half = jnp.where(core == 0, cr_s[...], cp_s[core])
    ren_o[...] = jnp.concatenate([first_half, second_half], axis=1).astype(BF16)

    wait_many(br, many_recv, 1)
    later = jnp.sum(jnp.where(number > cell, br[...], 0.0), axis=0)
    grad_depth = -jnp.concatenate([later[0:1], later[1:2]], axis=1)
    dg_o[...] = grad_depth
    after = jnp.sum(lit_slope, axis=0, keepdims=True) - ahead_of(lit_slope) - lit_slope
    grad_step = grad_depth + slope * (ahead * kept) - after
    grad_logit = grad_step * travel / (1.0 + jnp.exp(-logit))
    grad_second = None
    for k in range(SAMPLES):
        grad = weight[k:k + 1] * q_t[...] + grad_logit[k:k + 1] * wdb[...]
        grad = jnp.where(h2[k].astype(F32) > 0.0, grad, 0.0).astype(BF16)
        term = nt_dot(h1[k], grad)
        grad_second = term if k == 0 else grad_second + term
    gs_s[...] = grad_second.astype(BF16).reshape(gs_s.shape)
    to_groups(lambda t: gs_s.at[t], gs_r, 3)

    gf_r[group] = gf_s[group]
    gs_r[group] = gs_s[group]
    wait_many(gf_r, many_recv, 2)
    share_feature = jnp.sum(gf_r[...].astype(F32), axis=0)
    wait_many(gs_r, many_recv, 3)
    share_second = jnp.sum(gs_r[...].astype(F32), axis=0)
    share = jnp.concatenate([share_second, share_feature], axis=1)
    squares = jnp.sum(share * share, axis=0, keepdims=True)
    folded = squares[:, 0:HALF]
    for i in range(1, squares.shape[1] // HALF):
        folded = folded + squares[:, i * HALF:(i + 1) * HALF]
    sq[cell] = folded
    to_cells(sq, 4)
    ga[group] = share.astype(BF16)
    to_groups(lambda t: ga.at[group], ga, 5)
    wait_many(sq, many_recv, 4)
    sr[group] = jnp.sum(sq[...], axis=0)
    to_groups(lambda t: sr.at[group], sr, 6)
    for name in ("ms", "vs", "mf", "vf"):
        bring[name].wait()
    wait_many(ga, many_recv, 5)
    wait_many(sr, many_recv, 6)
    square_sum = jnp.sum(jnp.sum(sr[...], axis=0), axis=1, keepdims=True)
    entry_total = all_cells * width * (width + gp.shape[0])
    rescale = lax.rsqrt(square_sum / entry_total + mean_floor)

    def adam(gradient, mean_moment, square_moment):
        unit = gradient * rescale
        mean_new = beta_first * mean_moment + (1.0 - beta_first) * unit
        square_new = beta_second * square_moment + (1.0 - beta_second) * unit * unit
        return (mean_new / bias_first / (jnp.sqrt(square_new / bias_second) + adam_floor)).astype(BF16)

    per = ga.shape[1]

    def update(i, n):
        rows = pl.ds(pl.multiple_of(i * per, per), per)
        both = ga[i].astype(F32)
        us_o[rows, :] = adam(both[:, :width], ms_v[rows, :], vs_v[rows, :])
        uf_o[rows, :] = adam(both[:, width:], mf_v[rows, :], vf_v[rows, :])
        return n

    lax.fori_loop(0, n_rays, update, 0)

    for copy in sent:
        copy.wait_send()
    for i, buf in enumerate((dep, br, gf_r, gs_r, sq, ga, sr)):
        wait_many(buf, many_send, i)


def on_device(sizes, ray_code, entry_index, sample_count, step_length, positions, w_first, w_second,
              w_density, w_feature, mean_second, square_second, mean_feature, square_feature, target_color):
    n_z, n_y, n_x, _ = sizes
    n_cell, n_rays = 2 * n_z, n_y * n_x
    rows, width = ray_code.shape[0], ray_code.shape[2]
    table, channels = positions.shape[1], target_color.shape[1]
    part = channels // 16
    per = width // n_rays
    vmem = pltpu.VMEM
    args = (
        ray_code.reshape(rows, width), entry_index.reshape(1, rows), sample_count.reshape(1, rows),
        step_length.reshape(1, rows), positions[0], w_first[0], w_second[0], w_density,
        w_feature[0], mean_second[0], square_second[0], mean_feature[0], square_feature[0], target_color,
    )
    local = [vmem(a.shape, a.dtype) for a in args[:-1]] + [vmem((HALF, channels), BF16)]
    scratch = local + [
        vmem((width, rows), F32), vmem((width, table), BF16), vmem((width, width), BF16),
        vmem((width, width), BF16), vmem((channels, width), BF16), vmem((width, channels), BF16),
        vmem((width, rows), F32), vmem((SAMPLES, width, rows), BF16), vmem((SAMPLES, width, rows), BF16),
        vmem((SAMPLES, rows), F32), vmem((16, part, HALF), F32), vmem((width, rows), F32),
        vmem((channels, rows), BF16),
        vmem((n_cell, 2, HALF), F32), vmem((2, 2, HALF), F32), vmem((2, 16, part, HALF), BF16),
        vmem((16, part, HALF), BF16), vmem((4, 4, part, HALF), BF16), vmem((3, 4, part, HALF), BF16),
        vmem((4, part, HALF), BF16), vmem((3, part, HALF), BF16), vmem((2, part // 2, HALF), F32),
        vmem((part // 2, HALF), F32), vmem((2, 4, 4, part, HALF), BF16), vmem((n_cell, 2, HALF), F32),
        vmem((n_rays, per, channels), BF16), vmem((n_rays, per, channels), BF16),
        vmem((n_rays, per, width), BF16), vmem((n_rays, per, width), BF16),
        vmem((n_rays, per, width + channels), BF16), vmem((n_cell, 1, HALF), F32), vmem((n_rays, 1, HALF), F32),
        pltpu.SemaphoreType.DMA((14,)), pltpu.SemaphoreType.DMA((7,)), pltpu.SemaphoreType.DMA((7,)),
        pltpu.SemaphoreType.DMA((21,)), pltpu.SemaphoreType.DMA((21,)),
    ]
    rendered, depth_grad, update_second, update_feature = pl.pallas_call(
        functools.partial(kernel, sizes),
        out_shape=(
            jax.ShapeDtypeStruct((part // 2, rows), BF16),
            jax.ShapeDtypeStruct((1, rows), F32),
            jax.ShapeDtypeStruct((width, width), BF16),
            jax.ShapeDtypeStruct((width, channels), BF16),
        ),
        in_specs=[pl.BlockSpec(memory_space=pl.ANY)] * len(args),
        out_specs=[pl.BlockSpec(memory_space=vmem)] * 4,
        scratch_shapes=scratch,
        compiler_params=pltpu.CompilerParams(
            collective_id=0, has_side_effects=True, vmem_limit_bytes=62 * 1024 * 1024
        ),
    )(*args)
    return (rendered.T, depth_grad.reshape(rows, 1), update_second[None], update_feature[None])


def solution(mesh):
    n_cell, n_rays = mesh.devices.shape
    n_y = 4 if n_rays == 16 else 1
    sizes = (n_cell // 2, n_y, n_rays // n_y, n_cell)
    split = Mesh(mesh.devices.reshape(n_cell // 2, 2, n_y, n_rays // n_y), ("z", "core", "y", "x"))
    return jax.shard_map(
        functools.partial(on_device, sizes),
        mesh=split,
        in_specs=(
            P(RAYS, CELL, None),
            P(RAYS, CELL),
            P(RAYS, CELL),
            P(RAYS, CELL),
            P(CELL, None, None),
            P(CELL, None, None),
            P(CELL, None, None),
            P(CELL, None),
            P(CELL, None, None),
            P(CELL, None, None),
            P(CELL, None, None),
            P(CELL, None, None),
            P(CELL, None, None),
            P(RAYS, None),
        ),
        out_specs=(P(RAYS, CELL), P(RAYS, CELL), P(CELL, None, None), P(CELL, None, None)),
        check_vma=False,
    )
```

time: 283 us -> 81.8 us (0.29)
  the two profiles are of different devices: /device:TPU:8 before, /device:TPU:1 now
where the time goes in v1:
time: 81.8 us; the launch traced here: 81.6 us
  Pallas kernels  75.7 us (93%)
  local copies, waits for them, and re-layouts  5.26 us (6%)
    pallas_call x1, Pallas kernels, on_device(): pl.pallas_call(functools.partial(kernel, sizes), out_shape=(jax.ShapeDtyp...  75.7 us
    unnamed x8, local copies, waits for them, and re-layouts  5.26 us

profile of v1, /device:TPU:1, one launch (start us, length us, event | category | flops | bytes accessed | tf_op | source)
XLA Modules:
  0.0 81.6 jit_solution(10290001079376177778)
XLA Ops:
  0.6 75.7 %shard_map.165 = (bf16[24,256]{1,0:T(8,128)(2,1)}, f32[1,256]{1,0:T(1,128)}, bf16[256,256]{1,0:T(8,128)(2,1)}, bf16[256,768]{1,0:T(8,128)(2,1)}) custom-call(bf16[256,256]{1,0:T(8,128)(2,1)} %bitcast.23, s32[1,256]{1,0:T(1,128)} %bitcast.28, s32[1,256]{1,0:T(1,128)} %bitcast.29, f32[1,256]{1,0:T(1,128)} %bitcast.30, bf16[128,256]{1,0:T(8,128)(2,1)} %bitcast.26, ...), custom_call_target="tpu_custom_call" | custom-call | tf_op jit(solution)/shard_map/pallas_call | solution.py:370
  76.3 0.0 copy-start
  76.3 0.7 copy-done
  77.0 0.0 copy-start.1
  77.0 0.6 copy.22
  77.6 0.1 copy-done.1
  77.7 0.6 copy.23
  78.3 1.6 %copy.24 = bf16[1,256,256]{2,1,0:T(8,128)(2,1)} copy(bf16[1,256,256]{2,1,0:T(8,128)(2,1)} %bitcast.25) | data formatting | bytes 262144
  79.8 1.8 %copy.25 = bf16[1,256,768]{2,1,0:T(8,128)(2,1)} copy(bf16[1,256,768]{2,1,0:T(8,128)(2,1)} %bitcast.19) | data formatting | bytes 786432
Async XLA Ops:
  76.3 0.7 copy-start
  77.0 0.7 copy-start.1

commit v2 on v1

v2 whole, which is shorter than its diff:
```python
import functools

import jax
import jax.numpy as jnp
from jax import lax
from jax.experimental import pallas as pl
from jax.experimental.pallas import tpu as pltpu
from jax.sharding import Mesh
from jax.sharding import PartitionSpec as P

SAMPLES = 8
MESH = pl.DeviceIdType.MESH
CELL = ("z", "core")
RAYS = ("y", "x")
HALF = 128
F32 = jnp.float32
BF16 = jnp.bfloat16

beta_first = 0.9
beta_second = 0.999
bias_first = 0.19
bias_second = 0.001999
adam_floor = 1e-08
mean_floor = 1e-06


def nt_dot(a, b):
    return lax.dot_general(a, b, (((1,), (1,)), ((), ())), preferred_element_type=F32)


def mm(a, b):
    return jnp.dot(a, b, preferred_element_type=F32)


def kernel(
    sizes,
    ray_h, ent_h, cnt_h, stp_h, pos_h, w1_h, w2_h, wd_h, wf_h,
    tgt_h,
    ren_o, dg_o, gs_o, gf_o, sum_o,
    ray_v, ent_v, cnt_v, stp_v, pos_v, w1_v, w2_v, wd_v, wf_v,
    tgt_v,
    rayt, post, w1t, w2t, wft, wfb, wdb, h1, h2, lg, tgt_t, q_t, gp,
    dep, tt, pl_s, pr_s, ns_s, nr_s, fs_s, fr_s, cp_s, cr_s, own_s, rs_s, br,
    gf_s, gf_r, gs_s, gs_r, fa_s, sa_s, sq, sr,
    loc, many_send, many_recv, one_send, one_recv, blk_send, blk_recv,
):
    n_z, n_y, n_x, _ = sizes
    n_cell, n_rays = 2 * n_z, n_y * n_x
    z, core = lax.axis_index("z"), lax.axis_index("core")
    y, x = lax.axis_index("y"), lax.axis_index("x")
    cell = 2 * z + core
    group = n_x * y + x
    quad, res = lax.div(z, 4), lax.rem(z, 4)
    other = 1 - core

    def cell_device(t):
        return (lax.div(t, 2), lax.rem(t, 2), y, x)

    def rays_device(t):
        return (z, core, lax.div(t, n_x), lax.rem(t, n_x))

    def chip_device(t):
        return (lax.rem(t + n_z, n_z), core, y, x)

    sibling = (z, other, y, x)

    def each_cell(send):
        def step(j, n):
            to = lax.rem(z + 1 + lax.rem(lax.div(j, 2) + n_z // 2 - 2, n_z - 1), n_z)
            send(2 * to + lax.rem(j, 2))
            return n

        lax.fori_loop(0, n_cell - 2, step, 0)

    def each_group(send):
        def step(j, n):
            to_y = lax.rem(y + lax.div(j, n_x), n_y)
            to_x = lax.rem(x + lax.rem(j, n_x), n_x)
            send(to_y * n_x + to_x)
            return n

        lax.fori_loop(1, n_rays, step, 0)

    bring = {}
    for i, (name, src, dst) in enumerate((
        ("ent", ent_h, ent_v), ("pos", pos_h, pos_v), ("ray", ray_h, ray_v), ("w1", w1_h, w1_v),
        ("w2", w2_h, w2_v), ("wd", wd_h, wd_v), ("cnt", cnt_h, cnt_v), ("stp", stp_h, stp_v),
        ("wf", wf_h, wf_v),
        ("tgt", tgt_h.at[pl.ds(pl.multiple_of(core * HALF, HALF), HALF), :], tgt_v),
    )):
        bring[name] = pltpu.make_async_copy(src, dst, loc.at[i])
        bring[name].start()

    barrier = pltpu.get_barrier_semaphore()
    each_cell(lambda t: pl.semaphore_signal(barrier, inc=1, device_id=cell_device(t), device_id_type=MESH))
    pl.semaphore_signal(barrier, inc=1, device_id=sibling, device_id_type=MESH)
    each_group(lambda t: pl.semaphore_signal(barrier, inc=1, device_id=rays_device(t), device_id_type=MESH))

    for name in ("ent", "pos", "ray", "w1"):
        bring[name].wait()
    post[...] = pos_v[...].astype(F32).T.astype(BF16)
    rayt[...] = ray_v[...].astype(F32).T
    w1t[...] = w1_v[...].astype(F32).T.astype(BF16)
    for name in ("w2", "wd", "cnt", "stp"):
        bring[name].wait()
    w2t[...] = w2_v[...].T.astype(BF16)
    width = wd_v.shape[1]
    n_rows = ray_v.shape[0]
    wdb[...] = jnp.broadcast_to(wd_v[...].astype(F32), (n_rows, width)).T
    slot = lax.broadcasted_iota(jnp.int32, (pos_v.shape[0], n_rows), 0)

    def forward(k):
        hot = jnp.where(slot == ent_v[...] + k, 1.0, 0.0).astype(BF16)
        inputs = (mm(post[...], hot) + rayt[...]).astype(BF16)
        first = jnp.maximum(mm(w1t[...], inputs), 0.0).astype(BF16)
        second = jnp.maximum(mm(w2t[...], first), 0.0).astype(BF16)
        h1[k] = first
        h2[k] = second
        lg[pl.ds(k, 1), :] = jnp.sum(second.astype(F32) * wdb[...], axis=0, keepdims=True)

    def two(i, n):
        forward(2 * i)
        forward(2 * i + 1)
        return n

    lax.fori_loop(0, SAMPLES // 2, two, 0)

    order = lax.broadcasted_iota(jnp.int32, (SAMPLES, n_rows), 0)
    logit = lg[...]
    travel = jnp.where(order < cnt_v[...], stp_v[...], 0.0)
    step_depth = (jnp.maximum(logit, 0.0) + jnp.log1p(jnp.exp(-jnp.abs(logit)))) * travel

    def ahead_of(v):
        total = v
        for shift in (1, 2, 4):
            total = total + jnp.where(order >= shift, pltpu.roll(total, shift, 0), 0.0)
        return total - v

    ahead = jnp.exp(-ahead_of(step_depth))
    kept = jnp.exp(-step_depth)
    weight = ahead * (1.0 - kept)
    depth = jnp.sum(step_depth, axis=0, keepdims=True)

    def put_rows(buf, at, row):
        for half in range(2):
            buf[at, pl.ds(half, 1), :] = row[:, half * HALF:(half + 1) * HALF]

    put_rows(dep, cell, depth)
    pl.semaphore_wait(barrier, n_cell - 1 + n_rays - 1)

    def to_cells(buf, i):
        each_cell(lambda t: pltpu.make_async_remote_copy(
            buf.at[cell], buf.at[cell], many_send.at[i], many_recv.at[i],
            device_id=cell_device(t), device_id_type=MESH).start())

    def to_groups(src, dst, i):
        each_group(lambda t: pltpu.make_async_remote_copy(
            src(t), dst.at[group], many_send.at[i], many_recv.at[i],
            device_id=rays_device(t), device_id_type=MESH).start())

    def wait_many(buf, sem, i, left_out):
        part = buf.at[pl.ds(0, buf.shape[0] - left_out)]
        pltpu.make_async_copy(part, part, sem.at[i]).wait()

    sent, blocks = [], []

    def send(src, dst, i, device):
        copy = pltpu.make_async_remote_copy(
            src, dst, one_send.at[i], one_recv.at[i], device_id=device, device_id_type=MESH)
        copy.start()
        sent.append(copy)

    def arrived(dst, i):
        pltpu.make_async_copy(dst, dst, one_recv.at[i]).wait()

    def send_block(src, dst, i, at, device):
        copy = pltpu.make_async_remote_copy(
            src, dst, blk_send.at[len(blocks)], blk_recv.at[i, at], device_id=device, device_id_type=MESH)
        copy.start()
        sent.append(copy)
        blocks.append(copy)

    def block_arrived(dst, i, at):
        pltpu.make_async_copy(dst, dst, blk_recv.at[i, at]).wait()

    send(dep.at[cell], dep.at[cell], 5, sibling)
    to_cells(dep, 0)

    gather = weight[0:1] * h2[0].astype(F32)
    for k in range(1, SAMPLES):
        gather = gather + weight[k:k + 1] * h2[k].astype(F32)
    gathered = gather.astype(BF16)
    bring["wf"].wait()
    wfb[...] = wf_v[...].astype(BF16)
    wft[...] = wf_v[...].T.astype(BF16)
    partial = mm(wft[...], gathered).astype(BF16)
    for half in range(2):
        pl_s[half] = partial[:, half * HALF:(half + 1) * HALF].reshape(pl_s.shape[1:])
    send(pl_s.at[other], pr_s, 0, sibling)

    arrived(dep.at[2 * z + other], 5)
    nearer = jnp.exp(-dep[2 * z, pl.ds(core, 1), :])
    mine = jnp.where(core == 0, 1.0, nearer)
    theirs = jnp.where(core == 0, nearer, 1.0)
    arrived(pr_s, 0)
    for i in range(16):
        ns_s[i // 4, i % 4] = (mine * pl_s[core, i].astype(F32) + theirs * pr_s[i].astype(F32)).astype(BF16)

    def turn(a):
        return lax.rem(res + a + 4, 4)

    across = turn(2)
    send(ns_s.at[:, turn(3)], nr_s.at[0], 1, chip_device(z + 1))
    send(ns_s.at[:, turn(1)], nr_s.at[1], 2, chip_device(z - 1))
    send(ns_s.at[pl.ds(0, 2), res], nr_s.at[2, pl.ds(0, 2)], 3, chip_device(z + 2))
    send(ns_s.at[pl.ds(2, 2), res], nr_s.at[2, pl.ds(2, 2)], 4, chip_device(z - 2))
    bring["tgt"].wait()
    tgt_t[...] = tgt_v[...].astype(F32).T.reshape(tgt_t.shape)

    wait_many(dep, many_recv, 0, 2)
    number = lax.broadcasted_iota(jnp.int32, dep.shape, 0)
    depths = dep[...]

    def light(end):
        return jnp.exp(-jnp.sum(jnp.where(number < end, depths, 0.0), axis=0))

    for i, a in enumerate((0, -1, 1, -2, 2)):
        tt[i] = light(2 * lax.rem(z + a + n_z, n_z))
    tt[5] = light(cell)
    lights = [tt[i, pl.ds(core, 1), :] for i in range(5)]
    arrived(nr_s.at[0], 1)
    arrived(nr_s.at[1], 2)
    arrived(nr_s.at[2, pl.ds(0, 2)], 3)
    arrived(nr_s.at[2, pl.ds(2, 2)], 4)
    for i in range(4):
        fs_s[i] = (
            lights[0] * ns_s[i, across].astype(F32) + lights[1] * nr_s[0, i].astype(F32)
            + lights[2] * nr_s[1, i].astype(F32) + lights[3 + i // 2] * nr_s[2, i].astype(F32)
        ).astype(BF16)
    for a in (6, -6, 2, -2):
        to = lax.rem(z + a + n_z, n_z)
        send_block(fs_s.at[lax.div(to, 4)], fr_s.at[quad], 0, quad, chip_device(to))
    for i in range(4):
        block_arrived(fr_s.at[i], 0, i)
    lit = fr_s[0].astype(F32) + fr_s[1].astype(F32) + fr_s[2].astype(F32) + fr_s[3].astype(F32)

    own_s[...] = (lit - tgt_t[z]).astype(BF16)
    for a in (6, -6, 2, -2):
        send_block(own_s, rs_s.at[core, quad, res], 1, quad, chip_device(z + a + n_z))
    cp_s[...] = lit.reshape(cp_s.shape)
    send(cp_s.at[other], cr_s, 6, sibling)
    for a in (2, -2, 6, -6):
        at = lax.div(lax.rem(z + a + n_z, n_z), 4)
        block = rs_s.at[core, at, across]
        block_arrived(block, 1, at)
        send_block(block, block, 2, at, chip_device(z + 1))
        send_block(block, block, 3, at, chip_device(z - 1))
        send_block(block, block, 4, at, chip_device(z + 2 + 12 * lax.div(at, 2)))
        send_block(block, block, 5, at, sibling)
    for a in (2, -2, 6, -6):
        for i, beside, which in ((2, -1, turn(1)), (3, 1, turn(3)), (4, 2, res)):
            at = lax.div(lax.rem(z + beside + a + n_z, n_z), 4)
            block = rs_s.at[core, at, which]
            block_arrived(block, i, at)
            send_block(block, block, 4 + i, at, sibling)
    for i, which in ((5, across), (6, turn(1)), (7, turn(3)), (8, res)):
        for at in range(4):
            block_arrived(rs_s.at[other, at, which], i, at)

    transmit = tt[5]
    for half in range(2):
        block = rs_s[half].reshape(gp.shape[0], HALF).astype(F32)
        gp[:, half * HALF:(half + 1) * HALF] = (block * transmit[half:half + 1]).astype(BF16)
    q_t[...] = mm(wfb[...], gp[...])
    slopes = []
    for k in range(SAMPLES):
        slopes.append(jnp.sum(h2[k].astype(F32) * q_t[...], axis=0, keepdims=True))
    slope = jnp.concatenate(slopes, axis=0)
    lit_slope = weight * slope
    put_rows(br, cell, jnp.sum(lit_slope, axis=0, keepdims=True))
    send(br.at[cell], br.at[cell], 7, sibling)
    to_cells(br, 1)
    gf_s[...] = nt_dot(gathered, gp[...]).astype(BF16).reshape(gf_s.shape)
    to_groups(lambda t: gf_s.at[t], gf_r, 2)

    arrived(cr_s, 6)
    first_half = jnp.where(core == 0, cp_s[core], cr_s[...])
    second_half = jnp.where(core == 0, cr_s[...], cp_s[core])
    ren_o[...] = jnp.concatenate([first_half, second_half], axis=1).astype(BF16)
    gf_r[group] = gf_s[group]
    after = jnp.sum(lit_slope, axis=0, keepdims=True) - ahead_of(lit_slope) - lit_slope
    slope_step = slope * (ahead * kept) - after
    slope_scale = travel / (1.0 + jnp.exp(-logit))

    arrived(br.at[2 * z + other], 7)
    wait_many(br, many_recv, 1, 2)
    later = jnp.sum(jnp.where(number > cell, br[...], 0.0), axis=0)
    grad_depth = -jnp.concatenate([later[0:1], later[1:2]], axis=1)
    dg_o[...] = grad_depth
    grad_logit = (grad_depth + slope_step) * slope_scale
    grad_second = None
    for k in range(SAMPLES):
        grad = weight[k:k + 1] * q_t[...] + grad_logit[k:k + 1] * wdb[...]
        grad = jnp.where(h2[k].astype(F32) > 0.0, grad, 0.0).astype(BF16)
        term = nt_dot(h1[k], grad)
        grad_second = term if k == 0 else grad_second + term
    gs_s[...] = grad_second.astype(BF16).reshape(gs_s.shape)
    to_groups(lambda t: gs_s.at[t], gs_r, 3)
    gs_r[group] = gs_s[group]

    def folded(share):
        squares = jnp.sum(share * share, axis=0, keepdims=True)
        return sum(squares[:, i:i + HALF] for i in range(0, squares.shape[1], HALF))

    wait_many(gf_r, many_recv, 2, 1)
    share_feature = jnp.sum(gf_r[...].astype(F32), axis=0)
    square_feature = folded(share_feature)
    fa_s[...] = share_feature.astype(BF16)
    to_groups(lambda t: fa_s, gf_o, 5)
    own_feature = pltpu.make_async_copy(fa_s, gf_o.at[group], loc.at[10])
    own_feature.start()
    wait_many(gs_r, many_recv, 3, 1)
    share_second = jnp.sum(gs_r[...].astype(F32), axis=0)
    sq[cell] = square_feature + folded(share_second)
    send(sq.at[cell], sq.at[cell], 8, sibling)
    to_cells(sq, 4)
    sa_s[...] = share_second.astype(BF16)
    to_groups(lambda t: sa_s, gs_o, 6)
    own_second = pltpu.make_async_copy(sa_s, gs_o.at[group], loc.at[11])
    own_second.start()
    arrived(sq.at[2 * z + other], 8)
    wait_many(sq, many_recv, 4, 2)
    sr[group] = jnp.sum(sq[...], axis=0)
    to_groups(lambda t: sr.at[group], sr, 7)
    wait_many(gf_o, many_recv, 5, 1)
    wait_many(gs_o, many_recv, 6, 1)
    own_feature.wait()
    own_second.wait()
    for copy in sent:
        copy.wait_send()
    for i, (buf, left_out) in enumerate((
        (dep, 2), (br, 2), (gf_r, 1), (gs_r, 1), (sq, 2), (gf_o, 1), (gs_o, 1), (sr, 1),
    )):
        wait_many(buf, many_send, i, left_out)
    wait_many(sr, many_recv, 7, 1)
    sum_o[...] = jnp.sum(sr[...], axis=0)


def adam_kernel(
    entries,
    ren_h, dg_h, gs_h, gf_h, sum_h, ms_h, vs_h, mf_h, vf_h,
    ren_o, dg_o, us_o, uf_o,
    gs_v, gf_v, sum_v, ms_v, vs_v, mf_v, vf_v, us_v, uf_v,
    sem, feed, drain,
):
    n_rays, per, _ = gs_v.shape
    parts = feed.shape[0]
    groups, rows = n_rays // parts, per * n_rays // parts
    start = []
    for i, (src, dst) in enumerate((
        (sum_h, sum_v), (gs_h, gs_v), (ms_h, ms_v), (vs_h, vs_v), (ren_h, ren_o), (dg_h, dg_o),
    )):
        copy = pltpu.make_async_copy(src, dst, sem.at[i])
        copy.start()
        start.append(copy)
    fed = []
    for i in range(parts):
        some, block = pl.ds(i * rows, rows), pl.ds(i * groups, groups)
        copies = [
            pltpu.make_async_copy(gf_h.at[block], gf_v.at[block], feed.at[i, 0]),
            pltpu.make_async_copy(mf_h.at[some], mf_v.at[some], feed.at[i, 1]),
            pltpu.make_async_copy(vf_h.at[some], vf_v.at[some], feed.at[i, 2]),
        ]
        for copy in copies:
            copy.start()
        fed.append(copies)
    for copy in start[:4]:
        copy.wait()
    square_sum = jnp.sum(sum_v[...], axis=1, keepdims=True)
    rescale = lax.rsqrt(square_sum / entries + mean_floor)

    def adam(gradient, mean_moment, square_moment):
        unit = gradient.astype(F32) * rescale
        mean_new = beta_first * mean_moment + (1.0 - beta_first) * unit
        square_new = beta_second * square_moment + (1.0 - beta_second) * unit * unit
        return (mean_new / bias_first / (jnp.sqrt(square_new / bias_second) + adam_floor)).astype(BF16)

    def second(i, n):
        at = pl.ds(pl.multiple_of(i * per, per), per)
        us_v[at, :] = adam(gs_v[i], ms_v[at, :], vs_v[at, :])
        return n

    def feature(i, n):
        at = pl.ds(pl.multiple_of(i * per, per), per)
        uf_v[at, :] = adam(gf_v[i], mf_v[at, :], vf_v[at, :])
        return n

    lax.fori_loop(0, n_rays, second, 0)
    out = [pltpu.make_async_copy(us_v, us_o, sem.at[6])]
    out[0].start()
    for i in range(parts):
        for copy in fed[i]:
            copy.wait()
        lax.fori_loop(i * groups, (i + 1) * groups, feature, 0)
        some = pl.ds(i * rows, rows)
        out.append(pltpu.make_async_copy(uf_v.at[some], uf_o.at[some], drain.at[i]))
        out[-1].start()
    for copy in out + start[4:]:
        copy.wait()


def on_device(sizes, ray_code, entry_index, sample_count, step_length, positions, w_first, w_second,
              w_density, w_feature, mean_second, square_second, mean_feature, square_feature, target_color):
    n_z, n_y, n_x, all_cells = sizes
    n_cell, n_rays = 2 * n_z, n_y * n_x
    rows, width = ray_code.shape[0], ray_code.shape[2]
    table, channels = positions.shape[1], target_color.shape[1]
    part = channels // 16
    per = width // n_rays
    vmem = pltpu.VMEM
    args = (
        ray_code.reshape(rows, width), entry_index.reshape(1, rows), sample_count.reshape(1, rows),
        step_length.reshape(1, rows), positions[0], w_first[0], w_second[0], w_density,
        w_feature[0], target_color,
    )
    moments = (mean_second[0], square_second[0], mean_feature[0], square_feature[0])
    local = [vmem(a.shape, a.dtype) for a in args[:-1]] + [vmem((HALF, channels), BF16)]
    scratch = local + [
        vmem((width, rows), F32), vmem((width, table), BF16), vmem((width, width), BF16),
        vmem((width, width), BF16), vmem((channels, width), BF16), vmem((width, channels), BF16),
        vmem((width, rows), F32), vmem((SAMPLES, width, rows), BF16), vmem((SAMPLES, width, rows), BF16),
        vmem((SAMPLES, rows), F32), vmem((16, part, HALF), F32), vmem((width, rows), F32),
        vmem((channels, rows), BF16),
        vmem((n_cell, 2, HALF), F32), vmem((6, 2, HALF), F32), vmem((2, 16, part, HALF), BF16),
        vmem((16, part, HALF), BF16), vmem((4, 4, part, HALF), BF16), vmem((3, 4, part, HALF), BF16),
        vmem((4, part, HALF), BF16), vmem((4, part, HALF), BF16), vmem((2, part // 2, HALF), F32),
        vmem((part // 2, HALF), F32), vmem((part, HALF), BF16), vmem((2, 4, 4, part, HALF), BF16), vmem((n_cell, 2, HALF), F32),
        vmem((n_rays, per, channels), BF16), vmem((n_rays, per, channels), BF16),
        vmem((n_rays, per, width), BF16), vmem((n_rays, per, width), BF16),
        vmem((per, channels), BF16), vmem((per, width), BF16), vmem((n_cell, 1, HALF), F32), vmem((n_rays, 1, HALF), F32),
        pltpu.SemaphoreType.DMA((12,)), pltpu.SemaphoreType.DMA((8,)), pltpu.SemaphoreType.DMA((8,)),
        pltpu.SemaphoreType.DMA((9,)), pltpu.SemaphoreType.DMA((9,)),
        pltpu.SemaphoreType.DMA((36,)), pltpu.SemaphoreType.DMA((9, 4)),
    ]
    anywhere = pl.BlockSpec(memory_space=pl.ANY)
    inside = pl.BlockSpec(memory_space=vmem)
    found = pl.pallas_call(
        functools.partial(kernel, sizes),
        out_shape=(
            jax.ShapeDtypeStruct((part // 2, rows), BF16),
            jax.ShapeDtypeStruct((1, rows), F32),
            jax.ShapeDtypeStruct((n_rays, per, width), BF16),
            jax.ShapeDtypeStruct((n_rays, per, channels), BF16),
            jax.ShapeDtypeStruct((1, HALF), F32),
        ),
        in_specs=[anywhere] * len(args),
        out_specs=[inside, inside, anywhere, anywhere, inside],
        scratch_shapes=scratch,
        compiler_params=pltpu.CompilerParams(
            collective_id=0, has_side_effects=True, vmem_limit_bytes=62 * 1024 * 1024
        ),
    )(*args)
    parts = 4
    rendered, depth_grad, update_second, update_feature = pl.pallas_call(
        functools.partial(adam_kernel, all_cells * width * (width + channels)),
        out_shape=(
            jax.ShapeDtypeStruct((part // 2, rows), BF16),
            jax.ShapeDtypeStruct((1, rows), F32),
            jax.ShapeDtypeStruct((width, width), BF16),
            jax.ShapeDtypeStruct((width, channels), BF16),
        ),
        in_specs=[anywhere] * 9,
        out_specs=[anywhere] * 4,
        scratch_shapes=[
            vmem((n_rays, per, width), BF16), vmem((n_rays, per, channels), BF16), vmem((1, HALF), F32),
            *(vmem(m.shape, F32) for m in moments),
            vmem((width, width), BF16), vmem((width, channels), BF16),
            pltpu.SemaphoreType.DMA((7,)), pltpu.SemaphoreType.DMA((parts, 3)), pltpu.SemaphoreType.DMA((parts,)),
        ],
        compiler_params=pltpu.CompilerParams(vmem_limit_bytes=62 * 1024 * 1024),
    )(*found, *moments)
    return (rendered.T, depth_grad.reshape(rows, 1), update_second[None], update_feature[None])


def solution(mesh):
    n_cell, n_rays = mesh.devices.shape
    n_y = 4 if n_rays == 16 else 1
    sizes = (n_cell // 2, n_y, n_rays // n_y, n_cell)
    split = Mesh(mesh.devices.reshape(n_cell // 2, 2, n_y, n_rays // n_y), ("z", "core", "y", "x"))
    return jax.shard_map(
        functools.partial(on_device, sizes),
        mesh=split,
        in_specs=(
            P(RAYS, CELL, None),
            P(RAYS, CELL),
            P(RAYS, CELL),
            P(RAYS, CELL),
            P(CELL, None, None),
            P(CELL, None, None),
            P(CELL, None, None),
            P(CELL, None),
            P(CELL, None, None),
            P(CELL, None, None),
            P(CELL, None, None),
            P(CELL, None, None),
            P(CELL, None, None),
            P(RAYS, None),
        ),
        out_specs=(P(RAYS, CELL), P(RAYS, CELL), P(CELL, None, None), P(CELL, None, None)),
        check_vma=False,
    )
```

time: 81.8 us -> 72.5 us (0.89)
  local copies, waits for them, and re-layouts: 5.26 us -> 0 us
  Pallas kernels: 75.7 us -> 71.7 us
    pallas_call x1, Pallas kernels: 75.7 us -> 68.5 us  [on_device(): pl.pallas_call(functools.partial(kernel, sizes), out_shape=(jax.ShapeDtyp...]
    unnamed x8 -> x0, local copies, waits for them, and re-layouts: 5.26 us -> none
    pallas_call x0 -> x1, Pallas kernels: none -> 3.22 us  [on_device(): pl.pallas_call(functools.partial(adam_kernel, all_cells * width * (width...]
where the time goes in v2:
time: 72.5 us; the launch traced here: 72.3 us
  Pallas kernels  71.7 us (99%)
    pallas_call x1, Pallas kernels, on_device(): pl.pallas_call(functools.partial(kernel, sizes), out_shape=(jax.ShapeDtyp...  68.5 us
    pallas_call x1, Pallas kernels, on_device(): pl.pallas_call(functools.partial(adam_kernel, all_cells * width * (width...  3.22 us

profile of v2, /device:TPU:1, one launch (start us, length us, event | category | flops | bytes accessed | tf_op | source)
XLA Modules:
  0.0 72.3 jit_solution(50900677233042112)
XLA Ops:
  0.6 68.5 %shard_map.165 = (bf16[24,256]{1,0:T(8,128)(2,1)}, f32[1,256]{1,0:T(1,128)}, bf16[16,16,256]{2,1,0:T(8,128)(2,1)}, bf16[16,16,768]{2,1,0:T(8,128)(2,1)}, f32[1,128]{1,0:T(1,128)}) custom-call(bf16[256,256]{1,0:T(8,128)(2,1)} %bitcast.22, s32[1,256]{1,0:T(1,128)} %bitcast.25, s32[1,256]{1,0:T(1,128)} %bitcast.26, f32[1,256]{1,0:T(1,128)} %bitcast.27, ...), custom_call_target="tpu_custom_call" | custom-call | tf_op jit(solution)/shard_map/pallas_call | solution.py:447
  69.1 3.2 %shard_map.166 = (bf16[24,256]{1,0:T(8,128)(2,1)}, f32[1,256]{1,0:T(1,128)}, bf16[256,256]{1,0:T(8,128)(2,1)}, bf16[256,768]{1,0:T(8,128)(2,1)}) custom-call(bf16[24,256]{1,0:T(8,128)(2,1)} %get-tuple-element.13.ren_h, f32[1,256]{1,0:T(1,128)} %get-tuple-element.14.dg_h, bf16[16,16,256]{2,1,0:T(8,128)(2,1)} %get-tuple-element.15.gs_h, ...), custom_call_target="tpu_custom_call" | custom-call | tf_op jit(solution)/shard_map/pallas_call | solution.py:464

commit v3 on v2

--- a/solution.py
+++ b/solution.py
@@ -40,7 +40,7 @@
     ray_v, ent_v, cnt_v, stp_v, pos_v, w1_v, w2_v, wd_v, wf_v,
     tgt_v,
     rayt, post, w1t, w2t, wft, wfb, wdb, h1, h2, lg, tgt_t, q_t, gp,
-    dep, tt, pl_s, pr_s, ns_s, nr_s, fs_s, fr_s, cp_s, cr_s, own_s, rs_s, br,
+    dep, tt, pl_s, pr_s, ns_s, nr_s, fs_s, fr_s, cp_s, cr_s, own_s, rs_s, br, pb, rb, lp,
     gf_s, gf_r, gs_s, gs_r, fa_s, sa_s, sq, sr,
     loc, many_send, many_recv, one_send, one_recv, blk_send, blk_recv,
 ):
@@ -257,6 +257,30 @@
         send_block(block, block, 3, at, chip_device(z - 1))
         send_block(block, block, 4, at, chip_device(z + 2 + 12 * lax.div(at, 2)))
         send_block(block, block, 5, at, sibling)
+    sources = ((0, 0), (-1, 1), (1, 2), (-2, 3), (2, 4))
+    lit_rows = [0.0] * 5
+    for i in range(4):
+        block = rs_s[core, i, across].astype(F32)
+        for j, piece in ((0, ns_s[i, across]), (1, nr_s[0, i]), (2, nr_s[1, i]), (3 + i // 2, nr_s[2, i])):
+            lit_rows[j] = lit_rows[j] + block * piece.astype(F32)
+    chip = lax.broadcasted_iota(jnp.int32, (n_z, HALF), 0)
+    behind = jnp.zeros((n_z, HALF), F32)
+    for a, j in sources:
+        row = lights[j] * jnp.sum(lit_rows[j], axis=0, keepdims=True)
+        behind = behind + jnp.where(chip < lax.rem(z + a + n_z, n_z), row, 0.0)
+    for i in range(n_z):
+        pb[i] = behind[i:i + 1]
+
+    def to_chip(j, n):
+        to = lax.rem(z + 1 + lax.rem(j + n_z // 2 - 1, n_z - 1), n_z)
+        pltpu.make_async_remote_copy(
+            pb.at[to], rb.at[z], many_send.at[1], many_recv.at[1],
+            device_id=(to, core, y, x), device_id_type=MESH).start()
+        return n
+
+    lax.fori_loop(0, n_z - 1, to_chip, 0)
+    rb[z] = pb[z]
+
     for a in (2, -2, 6, -6):
         for i, beside, which in ((2, -1, turn(1)), (3, 1, turn(3)), (4, 2, res)):
             at = lax.div(lax.rem(z + beside + a + n_z, n_z), 4)
@@ -277,9 +301,8 @@
         slopes.append(jnp.sum(h2[k].astype(F32) * q_t[...], axis=0, keepdims=True))
     slope = jnp.concatenate(slopes, axis=0)
     lit_slope = weight * slope
-    put_rows(br, cell, jnp.sum(lit_slope, axis=0, keepdims=True))
-    send(br.at[cell], br.at[cell], 7, sibling)
-    to_cells(br, 1)
+    put_rows(br, core, jnp.sum(lit_slope, axis=0, keepdims=True))
+    send(br.at[core], br.at[core], 7, sibling)
     gf_s[...] = nt_dot(gathered, gp[...]).astype(BF16).reshape(gf_s.shape)
     to_groups(lambda t: gf_s.at[t], gf_r, 2)
 
@@ -292,10 +315,13 @@
     slope_step = slope * (ahead * kept) - after
     slope_scale = travel / (1.0 + jnp.exp(-logit))
 
-    arrived(br.at[2 * z + other], 7)
-    wait_many(br, many_recv, 1, 2)
-    later = jnp.sum(jnp.where(number > cell, br[...], 0.0), axis=0)
-    grad_depth = -jnp.concatenate([later[0:1], later[1:2]], axis=1)
+    wait_many(rb, many_recv, 1, 1)
+    lp[core] = jnp.sum(rb[...], axis=0)
+    send(lp.at[core], lp.at[core], 9, sibling)
+    arrived(br.at[other], 7)
+    follower = jnp.where(core == 0, br[1], 0.0)
+    arrived(lp.at[other], 9)
+    grad_depth = -jnp.concatenate([lp[0] + follower[0:1], lp[1] + follower[1:2]], axis=1)
     dg_o[...] = grad_depth
     grad_logit = (grad_depth + slope_step) * slope_scale
     grad_second = None
@@ -339,7 +365,7 @@
     for copy in sent:
         copy.wait_send()
     for i, (buf, left_out) in enumerate((
-        (dep, 2), (br, 2), (gf_r, 1), (gs_r, 1), (sq, 2), (gf_o, 1), (gs_o, 1), (sr, 1),
+        (dep, 2), (rb, 1), (gf_r, 1), (gs_r, 1), (sq, 2), (gf_o, 1), (gs_o, 1), (sr, 1),
     )):
         wait_many(buf, many_send, i, left_out)
     wait_many(sr, many_recv, 7, 1)
@@ -434,12 +460,13 @@
         vmem((n_cell, 2, HALF), F32), vmem((6, 2, HALF), F32), vmem((2, 16, part, HALF), BF16),
         vmem((16, part, HALF), BF16), vmem((4, 4, part, HALF), BF16), vmem((3, 4, part, HALF), BF16),
         vmem((4, part, HALF), BF16), vmem((4, part, HALF), BF16), vmem((2, part // 2, HALF), F32),
-        vmem((part // 2, HALF), F32), vmem((part, HALF), BF16), vmem((2, 4, 4, part, HALF), BF16), vmem((n_cell, 2, HALF), F32),
+        vmem((part // 2, HALF), F32), vmem((part, HALF), BF16), vmem((2, 4, 4, part, HALF), BF16), vmem((2, 2, HALF), F32),
+        vmem((n_z, 1, HALF), F32), vmem((n_z, 1, HALF), F32), vmem((2, 1, HALF), F32),
         vmem((n_rays, per, channels), BF16), vmem((n_rays, per, channels), BF16),
         vmem((n_rays, per, width), BF16), vmem((n_rays, per, width), BF16),
         vmem((per, channels), BF16), vmem((per, width), BF16), vmem((n_cell, 1, HALF), F32), vmem((n_rays, 1, HALF), F32),
         pltpu.SemaphoreType.DMA((12,)), pltpu.SemaphoreType.DMA((8,)), pltpu.SemaphoreType.DMA((8,)),
-        pltpu.SemaphoreType.DMA((9,)), pltpu.SemaphoreType.DMA((9,)),
+        pltpu.SemaphoreType.DMA((10,)), pltpu.SemaphoreType.DMA((10,)),
         pltpu.SemaphoreType.DMA((36,)), pltpu.SemaphoreType.DMA((9, 4)),
     ]
     anywhere = pl.BlockSpec(memory_space=pl.ANY)
@@ -460,7 +487,7 @@
             collective_id=0, has_side_effects=True, vmem_limit_bytes=62 * 1024 * 1024
         ),
     )(*args)
-    parts = 4
+    parts = min(4, n_rays)
     rendered, depth_grad, update_second, update_feature = pl.pallas_call(
         functools.partial(adam_kernel, all_cells * width * (width + channels)),
         out_shape=(

time: 72.5 us -> 69.4 us (0.957)
  Pallas kernels: 71.7 us -> 68.7 us
    pallas_call x1, Pallas kernels: 68.5 us -> 65.4 us  [on_device(): pl.pallas_call(functools.partial(kernel, sizes), out_shape=(jax.ShapeDtyp...]
where the time goes in v3:
time: 69.4 us; the launch traced here: 69.3 us
  Pallas kernels  68.7 us (99%)
    pallas_call x1, Pallas kernels, on_device(): pl.pallas_call(functools.partial(kernel, sizes), out_shape=(jax.ShapeDtyp...  65.4 us
    pallas_call x1, Pallas kernels, on_device(): pl.pallas_call(functools.partial(adam_kernel, all_cells * width * (width...  3.22 us

profile of v3, /device:TPU:1, one launch (start us, length us, event | category | flops | bytes accessed | tf_op | source)
XLA Modules:
  0.0 69.3 jit_solution(4521758900247091602)
XLA Ops:
  0.6 65.4 %shard_map.165 = (bf16[24,256]{1,0:T(8,128)(2,1)}, f32[1,256]{1,0:T(1,128)}, bf16[16,16,256]{2,1,0:T(8,128)(2,1)}, bf16[16,16,768]{2,1,0:T(8,128)(2,1)}, f32[1,128]{1,0:T(1,128)}) custom-call(bf16[256,256]{1,0:T(8,128)(2,1)} %bitcast.22, s32[1,256]{1,0:T(1,128)} %bitcast.25, s32[1,256]{1,0:T(1,128)} %bitcast.26, f32[1,256]{1,0:T(1,128)} %bitcast.27, ...), custom_call_target="tpu_custom_call" | custom-call | tf_op jit(solution)/shard_map/pallas_call | solution.py:474
  66.1 3.2 %shard_map.166 = (bf16[24,256]{1,0:T(8,128)(2,1)}, f32[1,256]{1,0:T(1,128)}, bf16[256,256]{1,0:T(8,128)(2,1)}, bf16[256,768]{1,0:T(8,128)(2,1)}) custom-call(bf16[24,256]{1,0:T(8,128)(2,1)} %get-tuple-element.13.ren_h, f32[1,256]{1,0:T(1,128)} %get-tuple-element.14.dg_h, bf16[16,16,256]{2,1,0:T(8,128)(2,1)} %get-tuple-element.15.gs_h, ...), custom_call_target="tpu_custom_call" | custom-call | tf_op jit(solution)/shard_map/pallas_call | solution.py:491

commit v4 on v3

--- a/solution.py
+++ b/solution.py
@@ -39,7 +39,7 @@
     ren_o, dg_o, gs_o, gf_o, sum_o,
     ray_v, ent_v, cnt_v, stp_v, pos_v, w1_v, w2_v, wd_v, wf_v,
     tgt_v,
-    rayt, post, w1t, w2t, wft, wfb, wdb, h1, h2, lg, tgt_t, q_t, gp,
+    rayt, post, w2t, wft, wfb, wdb, h1, h2, lg, tgt_t, q_t, gp, gb,
     dep, tt, pl_s, pr_s, ns_s, nr_s, fs_s, fr_s, cp_s, cr_s, own_s, rs_s, br, pb, rb, lp,
     gf_s, gf_r, gs_s, gs_r, fa_s, sa_s, sq, sr,
     loc, many_send, many_recv, one_send, one_recv, blk_send, blk_recv,
@@ -64,22 +64,25 @@
 
     sibling = (z, other, y, x)
 
+    def away(i, n):
+        half = lax.div(i + 1, 2)
+        return n // 2 + half - 2 * half * lax.rem(i, 2)
+
     def each_cell(send):
         def step(j, n):
-            to = lax.rem(z + 1 + lax.rem(lax.div(j, 2) + n_z // 2 - 2, n_z - 1), n_z)
-            send(2 * to + lax.rem(j, 2))
+            send(2 * lax.rem(z + away(lax.div(j, 2), n_z), n_z) + lax.rem(j, 2))
             return n
 
         lax.fori_loop(0, n_cell - 2, step, 0)
 
     def each_group(send):
         def step(j, n):
-            to_y = lax.rem(y + lax.div(j, n_x), n_y)
-            to_x = lax.rem(x + lax.rem(j, n_x), n_x)
+            to_y = lax.rem(y + away(lax.div(j, n_x), n_y), n_y)
+            to_x = lax.rem(x + away(lax.rem(j, n_x), n_x), n_x)
             send(to_y * n_x + to_x)
             return n
 
-        lax.fori_loop(1, n_rays, step, 0)
+        lax.fori_loop(0, n_rays - 1, step, 0)
 
     bring = {}
     for i, (name, src, dst) in enumerate((
@@ -96,34 +99,28 @@
     pl.semaphore_signal(barrier, inc=1, device_id=sibling, device_id_type=MESH)
     each_group(lambda t: pl.semaphore_signal(barrier, inc=1, device_id=rays_device(t), device_id_type=MESH))
 
-    for name in ("ent", "pos", "ray", "w1"):
+    for name in ("pos", "ray", "w1"):
         bring[name].wait()
-    post[...] = pos_v[...].astype(F32).T.astype(BF16)
-    rayt[...] = ray_v[...].astype(F32).T
-    w1t[...] = w1_v[...].astype(F32).T.astype(BF16)
-    for name in ("w2", "wd", "cnt", "stp"):
+    width = wd_v.shape[1]
+    n_rows = ray_v.shape[0]
+    placed = mm(pos_v[...], w1_v[...]).T
+    coarse = placed.astype(BF16)
+    post[...] = jnp.concatenate([coarse, (placed - coarse.astype(F32)).astype(BF16)], axis=1)
+    rayt[...] = mm(ray_v[...], w1_v[...]).T
+    for name in ("w2", "wd", "ent", "cnt", "stp", "wf"):
         bring[name].wait()
     w2t[...] = w2_v[...].T.astype(BF16)
-    width = wd_v.shape[1]
-    n_rows = ray_v.shape[0]
-    wdb[...] = jnp.broadcast_to(wd_v[...].astype(F32), (n_rows, width)).T
+    column = jnp.broadcast_to(wd_v[...].astype(F32), (HALF, width)).T
+    wdb[...] = jnp.concatenate([column] * (n_rows // HALF), axis=1)
     slot = lax.broadcasted_iota(jnp.int32, (pos_v.shape[0], n_rows), 0)
-
-    def forward(k):
+    for k in range(SAMPLES):
         hot = jnp.where(slot == ent_v[...] + k, 1.0, 0.0).astype(BF16)
-        inputs = (mm(post[...], hot) + rayt[...]).astype(BF16)
-        first = jnp.maximum(mm(w1t[...], inputs), 0.0).astype(BF16)
+        hot = jnp.concatenate([hot, hot], axis=0)
+        first = jnp.maximum(mm(post[...], hot) + rayt[...], 0.0).astype(BF16)
         second = jnp.maximum(mm(w2t[...], first), 0.0).astype(BF16)
-        h1[k] = first
+        h1[:, k * n_rows:(k + 1) * n_rows] = first
         h2[k] = second
-        lg[pl.ds(k, 1), :] = jnp.sum(second.astype(F32) * wdb[...], axis=0, keepdims=True)
-
-    def two(i, n):
-        forward(2 * i)
-        forward(2 * i + 1)
-        return n
-
-    lax.fori_loop(0, SAMPLES // 2, two, 0)
+        lg[k:k + 1] = jnp.sum(second.astype(F32) * wdb[...], axis=0, keepdims=True)
 
     order = lax.broadcasted_iota(jnp.int32, (SAMPLES, n_rows), 0)
     logit = lg[...]
@@ -190,7 +187,6 @@
     for k in range(1, SAMPLES):
         gather = gather + weight[k:k + 1] * h2[k].astype(F32)
     gathered = gather.astype(BF16)
-    bring["wf"].wait()
     wfb[...] = wf_v[...].astype(BF16)
     wft[...] = wf_v[...].T.astype(BF16)
     partial = mm(wft[...], gathered).astype(BF16)
@@ -272,7 +268,7 @@
         pb[i] = behind[i:i + 1]
 
     def to_chip(j, n):
-        to = lax.rem(z + 1 + lax.rem(j + n_z // 2 - 1, n_z - 1), n_z)
+        to = lax.rem(z + away(j, n_z), n_z)
         pltpu.make_async_remote_copy(
             pb.at[to], rb.at[z], many_send.at[1], many_recv.at[1],
             device_id=(to, core, y, x), device_id_type=MESH).start()
@@ -324,13 +320,10 @@
     grad_depth = -jnp.concatenate([lp[0] + follower[0:1], lp[1] + follower[1:2]], axis=1)
     dg_o[...] = grad_depth
     grad_logit = (grad_depth + slope_step) * slope_scale
-    grad_second = None
     for k in range(SAMPLES):
         grad = weight[k:k + 1] * q_t[...] + grad_logit[k:k + 1] * wdb[...]
-        grad = jnp.where(h2[k].astype(F32) > 0.0, grad, 0.0).astype(BF16)
-        term = nt_dot(h1[k], grad)
-        grad_second = term if k == 0 else grad_second + term
-    gs_s[...] = grad_second.astype(BF16).reshape(gs_s.shape)
+        gb[:, k * n_rows:(k + 1) * n_rows] = jnp.where(h2[k].astype(F32) > 0.0, grad, 0.0).astype(BF16)
+    gs_s[...] = nt_dot(h1[...], gb[...]).astype(BF16).reshape(gs_s.shape)
     to_groups(lambda t: gs_s.at[t], gs_r, 3)
     gs_r[group] = gs_s[group]
 
@@ -383,9 +376,7 @@
     parts = feed.shape[0]
     groups, rows = n_rays // parts, per * n_rays // parts
     start = []
-    for i, (src, dst) in enumerate((
-        (sum_h, sum_v), (gs_h, gs_v), (ms_h, ms_v), (vs_h, vs_v), (ren_h, ren_o), (dg_h, dg_o),
-    )):
+    for i, (src, dst) in enumerate(((sum_h, sum_v), (ren_h, ren_o), (dg_h, dg_o))):
         copy = pltpu.make_async_copy(src, dst, sem.at[i])
         copy.start()
         start.append(copy)
@@ -393,15 +384,15 @@
     for i in range(parts):
         some, block = pl.ds(i * rows, rows), pl.ds(i * groups, groups)
         copies = [
-            pltpu.make_async_copy(gf_h.at[block], gf_v.at[block], feed.at[i, 0]),
-            pltpu.make_async_copy(mf_h.at[some], mf_v.at[some], feed.at[i, 1]),
-            pltpu.make_async_copy(vf_h.at[some], vf_v.at[some], feed.at[i, 2]),
+            pltpu.make_async_copy(gs_h.at[block], gs_v.at[block], feed.at[i, 0]),
+            pltpu.make_async_copy(gf_h.at[block], gf_v.at[block], feed.at[i, 5]),
         ]
+        for j, (src, dst) in enumerate(((ms_h, ms_v), (vs_h, vs_v), (mf_h, mf_v), (vf_h, vf_v))):
+            copies.append(pltpu.make_async_copy(src.at[some], dst.at[some], feed.at[i, 1 + j]))
         for copy in copies:
             copy.start()
         fed.append(copies)
-    for copy in start[:4]:
-        copy.wait()
+    start[0].wait()
     square_sum = jnp.sum(sum_v[...], axis=1, keepdims=True)
     rescale = lax.rsqrt(square_sum / entries + mean_floor)
 
@@ -409,29 +400,26 @@
         unit = gradient.astype(F32) * rescale
         mean_new = beta_first * mean_moment + (1.0 - beta_first) * unit
         square_new = beta_second * square_moment + (1.0 - beta_second) * unit * unit
-        return (mean_new / bias_first / (jnp.sqrt(square_new / bias_second) + adam_floor)).astype(BF16)
-
-    def second(i, n):
+        spread = square_new * (1.0 / bias_second)
+        spread = spread * lax.rsqrt(spread) + adam_floor
+        return (mean_new * (1.0 / bias_first) * pltpu.reciprocal(spread)).astype(BF16)
+
+    def update(i, n):
         at = pl.ds(pl.multiple_of(i * per, per), per)
         us_v[at, :] = adam(gs_v[i], ms_v[at, :], vs_v[at, :])
-        return n
-
-    def feature(i, n):
-        at = pl.ds(pl.multiple_of(i * per, per), per)
         uf_v[at, :] = adam(gf_v[i], mf_v[at, :], vf_v[at, :])
         return n
 
-    lax.fori_loop(0, n_rays, second, 0)
-    out = [pltpu.make_async_copy(us_v, us_o, sem.at[6])]
-    out[0].start()
+    out = []
     for i in range(parts):
         for copy in fed[i]:
             copy.wait()
-        lax.fori_loop(i * groups, (i + 1) * groups, feature, 0)
+        lax.fori_loop(i * groups, (i + 1) * groups, update, 0)
         some = pl.ds(i * rows, rows)
-        out.append(pltpu.make_async_copy(uf_v.at[some], uf_o.at[some], drain.at[i]))
-        out[-1].start()
-    for copy in out + start[4:]:
+        for j, (src, dst) in enumerate(((us_v, us_o), (uf_v, uf_o))):
+            out.append(pltpu.make_async_copy(src.at[some], dst.at[some], drain.at[i, j]))
+            out[-1].start()
+    for copy in out + start[1:]:
         copy.wait()
 
 
@@ -452,11 +440,11 @@
     moments = (mean_second[0], square_second[0], mean_feature[0], square_feature[0])
     local = [vmem(a.shape, a.dtype) for a in args[:-1]] + [vmem((HALF, channels), BF16)]
     scratch = local + [
-        vmem((width, rows), F32), vmem((width, table), BF16), vmem((width, width), BF16),
+        vmem((width, rows), F32), vmem((width, 2 * table), BF16),
         vmem((width, width), BF16), vmem((channels, width), BF16), vmem((width, channels), BF16),
-        vmem((width, rows), F32), vmem((SAMPLES, width, rows), BF16), vmem((SAMPLES, width, rows), BF16),
+        vmem((width, rows), F32), vmem((width, SAMPLES * rows), BF16), vmem((SAMPLES, width, rows), BF16),
         vmem((SAMPLES, rows), F32), vmem((16, part, HALF), F32), vmem((width, rows), F32),
-        vmem((channels, rows), BF16),
+        vmem((channels, rows), BF16), vmem((width, SAMPLES * rows), BF16),
         vmem((n_cell, 2, HALF), F32), vmem((6, 2, HALF), F32), vmem((2, 16, part, HALF), BF16),
         vmem((16, part, HALF), BF16), vmem((4, 4, part, HALF), BF16), vmem((3, 4, part, HALF), BF16),
         vmem((4, part, HALF), BF16), vmem((4, part, HALF), BF16), vmem((2, part // 2, HALF), F32),
@@ -502,7 +490,7 @@
             vmem((n_rays, per, width), BF16), vmem((n_rays, per, channels), BF16), vmem((1, HALF), F32),
             *(vmem(m.shape, F32) for m in moments),
             vmem((width, width), BF16), vmem((width, channels), BF16),
-            pltpu.SemaphoreType.DMA((7,)), pltpu.SemaphoreType.DMA((parts, 3)), pltpu.SemaphoreType.DMA((parts,)),
+            pltpu.SemaphoreType.DMA((3,)), pltpu.SemaphoreType.DMA((parts, 6)), pltpu.SemaphoreType.DMA((parts, 2)),
         ],
         compiler_params=pltpu.CompilerParams(vmem_limit_bytes=62 * 1024 * 1024),
     )(*found, *moments)

time: 69.4 us -> 66.8 us (0.963)
  Pallas kernels: 68.7 us -> 66 us
    pallas_call x1, Pallas kernels: 65.4 us -> 63 us  [on_device(): pl.pallas_call(functools.partial(kernel, sizes), out_shape=(jax.ShapeDtyp...]
where the time goes in v4:
time: 66.8 us; the launch traced here: 66.6 us
  Pallas kernels  66 us (99%)
    pallas_call x1, Pallas kernels, on_device(): pl.pallas_call(functools.partial(kernel, sizes), out_shape=(jax.ShapeDtyp...  63 us
    pallas_call x1, Pallas kernels, on_device(): pl.pallas_call(functools.partial(adam_kernel, all_cells * width * (width...  3.01 us

profile of v4, /device:TPU:1, one launch (start us, length us, event | category | flops | bytes accessed | tf_op | source)
XLA Modules:
  0.0 66.6 jit_solution(7191566806323299931)
XLA Ops:
  0.6 63.0 %shard_map.165 = (bf16[24,256]{1,0:T(8,128)(2,1)}, f32[1,256]{1,0:T(1,128)}, bf16[16,16,256]{2,1,0:T(8,128)(2,1)}, bf16[16,16,768]{2,1,0:T(8,128)(2,1)}, f32[1,128]{1,0:T(1,128)}) custom-call(bf16[256,256]{1,0:T(8,128)(2,1)} %bitcast.22, s32[1,256]{1,0:T(1,128)} %bitcast.25, s32[1,256]{1,0:T(1,128)} %bitcast.26, f32[1,256]{1,0:T(1,128)} %bitcast.27, ...), custom_call_target="tpu_custom_call" | custom-call | tf_op jit(solution)/shard_map/pallas_call | solution.py:462
  63.6 3.0 %shard_map.166 = (bf16[24,256]{1,0:T(8,128)(2,1)}, f32[1,256]{1,0:T(1,128)}, bf16[256,256]{1,0:T(8,128)(2,1)}, bf16[256,768]{1,0:T(8,128)(2,1)}) custom-call(bf16[24,256]{1,0:T(8,128)(2,1)} %get-tuple-element.13.ren_h, f32[1,256]{1,0:T(1,128)} %get-tuple-element.14.dg_h, bf16[16,16,256]{2,1,0:T(8,128)(2,1)} %get-tuple-element.15.gs_h, ...), custom_call_target="tpu_custom_call" | custom-call | tf_op jit(solution)/shard_map/pallas_call | solution.py:479

commit v5 on v4

--- a/solution.py
+++ b/solution.py
@@ -206,10 +206,10 @@
         return lax.rem(res + a + 4, 4)
 
     across = turn(2)
+    send(ns_s.at[pl.ds(0, 2), res], nr_s.at[2, pl.ds(0, 2)], 3, chip_device(z + 2))
+    send(ns_s.at[pl.ds(2, 2), res], nr_s.at[2, pl.ds(2, 2)], 4, chip_device(z - 2))
     send(ns_s.at[:, turn(3)], nr_s.at[0], 1, chip_device(z + 1))
     send(ns_s.at[:, turn(1)], nr_s.at[1], 2, chip_device(z - 1))
-    send(ns_s.at[pl.ds(0, 2), res], nr_s.at[2, pl.ds(0, 2)], 3, chip_device(z + 2))
-    send(ns_s.at[pl.ds(2, 2), res], nr_s.at[2, pl.ds(2, 2)], 4, chip_device(z - 2))
     bring["tgt"].wait()
     tgt_t[...] = tgt_v[...].astype(F32).T.reshape(tgt_t.shape)
 
@@ -249,9 +249,9 @@
         at = lax.div(lax.rem(z + a + n_z, n_z), 4)
         block = rs_s.at[core, at, across]
         block_arrived(block, 1, at)
+        send_block(block, block, 4, at, chip_device(z + 2 + 12 * lax.div(at, 2)))
         send_block(block, block, 2, at, chip_device(z + 1))
         send_block(block, block, 3, at, chip_device(z - 1))
-        send_block(block, block, 4, at, chip_device(z + 2 + 12 * lax.div(at, 2)))
         send_block(block, block, 5, at, sibling)
     sources = ((0, 0), (-1, 1), (1, 2), (-2, 3), (2, 4))
     lit_rows = [0.0] * 5

time: 66.8 us -> 66.4 us (level)
  no operation moved by 1% of the time
where the time goes in v5:
time: 66.4 us; the launch traced here: 66.2 us
  Pallas kernels  65.6 us (99%)
    pallas_call x1, Pallas kernels, on_device(): pl.pallas_call(functools.partial(kernel, sizes), out_shape=(jax.ShapeDtyp...  62.6 us
    pallas_call x1, Pallas kernels, on_device(): pl.pallas_call(functools.partial(adam_kernel, all_cells * width * (width...  3.01 us

profile of v5, /device:TPU:1, one launch (start us, length us, event | category | flops | bytes accessed | tf_op | source)
XLA Modules:
  0.0 66.2 jit_solution(13558840122253962855)
XLA Ops:
  0.6 62.6 %shard_map.165 = (bf16[24,256]{1,0:T(8,128)(2,1)}, f32[1,256]{1,0:T(1,128)}, bf16[16,16,256]{2,1,0:T(8,128)(2,1)}, bf16[16,16,768]{2,1,0:T(8,128)(2,1)}, f32[1,128]{1,0:T(1,128)}) custom-call(bf16[256,256]{1,0:T(8,128)(2,1)} %bitcast.22, s32[1,256]{1,0:T(1,128)} %bitcast.25, s32[1,256]{1,0:T(1,128)} %bitcast.26, f32[1,256]{1,0:T(1,128)} %bitcast.27, ...), custom_call_target="tpu_custom_call" | custom-call | tf_op jit(solution)/shard_map/pallas_call | solution.py:462
  63.2 3.0 %shard_map.166 = (bf16[24,256]{1,0:T(8,128)(2,1)}, f32[1,256]{1,0:T(1,128)}, bf16[256,256]{1,0:T(8,128)(2,1)}, bf16[256,768]{1,0:T(8,128)(2,1)}) custom-call(bf16[24,256]{1,0:T(8,128)(2,1)} %get-tuple-element.13.ren_h, f32[1,256]{1,0:T(1,128)} %get-tuple-element.14.dg_h, bf16[16,16,256]{2,1,0:T(8,128)(2,1)} %get-tuple-element.15.gs_h, ...), custom_call_target="tpu_custom_call" | custom-call | tf_op jit(solution)/shard_map/pallas_call | solution.py:479

commit v6 on v5

--- a/solution.py
+++ b/solution.py
@@ -299,6 +299,9 @@
     lit_slope = weight * slope
     put_rows(br, core, jnp.sum(lit_slope, axis=0, keepdims=True))
     send(br.at[core], br.at[core], 7, sibling)
+    wait_many(rb, many_recv, 1, 1)
+    lp[core] = jnp.sum(rb[...], axis=0)
+    send(lp.at[core], lp.at[core], 9, sibling)
     gf_s[...] = nt_dot(gathered, gp[...]).astype(BF16).reshape(gf_s.shape)
     to_groups(lambda t: gf_s.at[t], gf_r, 2)
 
@@ -311,9 +314,6 @@
     slope_step = slope * (ahead * kept) - after
     slope_scale = travel / (1.0 + jnp.exp(-logit))
 
-    wait_many(rb, many_recv, 1, 1)
-    lp[core] = jnp.sum(rb[...], axis=0)
-    send(lp.at[core], lp.at[core], 9, sibling)
     arrived(br.at[other], 7)
     follower = jnp.where(core == 0, br[1], 0.0)
     arrived(lp.at[other], 9)

time: 66.4 us -> 69.5 us (1.047)
  Pallas kernels: 65.6 us -> 68.7 us
    pallas_call x1, Pallas kernels: 62.6 us -> 65.7 us  [on_device(): pl.pallas_call(functools.partial(kernel, sizes), out_shape=(jax.ShapeDtyp...]
where the time goes in v6:
time: 69.5 us; the launch traced here: 69.4 us
  Pallas kernels  68.7 us (99%)
    pallas_call x1, Pallas kernels, on_device(): pl.pallas_call(functools.partial(kernel, sizes), out_shape=(jax.ShapeDtyp...  65.7 us
    pallas_call x1, Pallas kernels, on_device(): pl.pallas_call(functools.partial(adam_kernel, all_cells * width * (width...  3.01 us

profile of v6, /device:TPU:1, one launch (start us, length us, event | category | flops | bytes accessed | tf_op | source)
XLA Modules:
  0.0 69.4 jit_solution(11131195360670552137)
XLA Ops:
  0.6 65.7 %shard_map.165 = (bf16[24,256]{1,0:T(8,128)(2,1)}, f32[1,256]{1,0:T(1,128)}, bf16[16,16,256]{2,1,0:T(8,128)(2,1)}, bf16[16,16,768]{2,1,0:T(8,128)(2,1)}, f32[1,128]{1,0:T(1,128)}) custom-call(bf16[256,256]{1,0:T(8,128)(2,1)} %bitcast.22, s32[1,256]{1,0:T(1,128)} %bitcast.25, s32[1,256]{1,0:T(1,128)} %bitcast.26, f32[1,256]{1,0:T(1,128)} %bitcast.27, ...), custom_call_target="tpu_custom_call" | custom-call | tf_op jit(solution)/shard_map/pallas_call | solution.py:462
  66.4 3.0 %shard_map.166 = (bf16[24,256]{1,0:T(8,128)(2,1)}, f32[1,256]{1,0:T(1,128)}, bf16[256,256]{1,0:T(8,128)(2,1)}, bf16[256,768]{1,0:T(8,128)(2,1)}) custom-call(bf16[24,256]{1,0:T(8,128)(2,1)} %get-tuple-element.13.ren_h, f32[1,256]{1,0:T(1,128)} %get-tuple-element.14.dg_h, bf16[16,16,256]{2,1,0:T(8,128)(2,1)} %get-tuple-element.15.gs_h, ...), custom_call_target="tpu_custom_call" | custom-call | tf_op jit(solution)/shard_map/pallas_call | solution.py:479
